TPU v7x, 256 devices: a whole 4x4x8 slice. The times are simulated.
256 devices in a mesh: seq: 32 (over x, z_lo, core), dp: 8 (over y, z_hi).
Axes of the slice: x: 4, y: 4, z: 8 (z_hi: 2, z_lo: 4; z = z_hi * 4 + z_lo), core: 2. Of those that a mesh axis runs over, the one named last changes fastest.
Arguments:
- activations: bfloat16 [8, 32768, 256], P('dp', 'seq'), may hold values from -6 to 6
- gate_values: bfloat16 [8, 32768, 256], P('dp', 'seq'), may hold values from -6 to 6
- output_grad: bfloat16 [8, 32768, 256], P('dp', 'seq'), may hold values from -6 to 6
- filter_codes: bfloat16 [32768, 256], P('seq'), may hold values from -4 to 4
- filter_scales: float32 [256, 256], P('seq'), as said below
Outputs:
- input_grad: float32 [8, 32768, 256], P('dp', 'seq')
- gate_grad: bfloat16 [8, 32768, 256], P('dp', 'seq')
- code_grad: float32 [32768, 256], P('seq')
Inputs may be any that keep to these rules, and one draw needn't show every extreme that they name: `filter_scales`: every entry lies between 0.3 / sqrt(32768) and 3 / sqrt(32768).
All inputs are finite; a program needn't handle non-finite values.
Results may differ from a plain program's by a relative error of at most 0.001.
Values may be sent and summed in bfloat16 or wider, within the bound.
A program may use at most 128 MiB of HBM per device.

v0:
```python
import math

import jax
import jax.numpy as jnp
from jax import lax
from jax.sharding import PartitionSpec as P


def angle_table(period, row_count, col_count, direction):
    row_index = jnp.arange(row_count, dtype=jnp.int32)[:, None]
    col_index = jnp.arange(col_count, dtype=jnp.int32)[None, :]
    phase_angle = (row_index * col_index % period).astype(jnp.float32) * (2.0 * math.pi / period)
    return (jnp.cos(phase_angle), direction * jnp.sin(phase_angle))


def contract(pattern, left, right):
    return jnp.einsum(pattern, left, right, precision=lax.Precision.HIGHEST)


def complex_contract(pattern, left_re, left_im, right_re, right_im):
    real_part = contract(pattern, left_re, right_re) - contract(pattern, left_im, right_im)
    imag_part = contract(pattern, left_re, right_im) + contract(pattern, left_im, right_re)
    return (real_part, imag_part)


def factor_pair(whole_len):
    smaller = 1
    for divisor in range(1, math.isqrt(whole_len) + 1):
        if whole_len % divisor == 0:
            smaller = divisor
    return (smaller, whole_len // smaller)


def spectrum(signal, size_one, size_two):
    channels = signal.shape[0]
    blocks = signal.reshape(channels, size_one, size_two)
    outer_re, outer_im = angle_table(size_one, size_one, size_one, -1.0)
    section_re = contract("cab,ak->ckb", blocks, outer_re)
    section_im = contract("cab,ak->ckb", blocks, outer_im)
    twist_re, twist_im = angle_table(size_one * size_two, size_one, size_two, -1.0)
    turned_re = section_re * twist_re - section_im * twist_im
    turned_im = section_re * twist_im + section_im * twist_re
    inner_re, inner_im = angle_table(size_two, size_two, size_two, -1.0)
    return complex_contract("ckb,bm->ckm", turned_re, turned_im, inner_re, inner_im)


def signal_of(spec_re, spec_im, size_one, size_two):
    channels = spec_re.shape[0]
    inner_re, inner_im = angle_table(size_two, size_two, size_two, 1.0)
    section_re, section_im = complex_contract("ckm,mb->ckb", spec_re, spec_im, inner_re, inner_im)
    twist_re, twist_im = angle_table(size_one * size_two, size_one, size_two, 1.0)
    turned_re = section_re * twist_re - section_im * twist_im
    turned_im = section_re * twist_im + section_im * twist_re
    outer_re, outer_im = angle_table(size_one, size_one, size_one, 1.0)
    result = contract("ckb,ka->cab", turned_re, outer_re) - contract(
        "ckb,ka->cab", turned_im, outer_im
    )
    return result.reshape(channels, size_one * size_two) / float(size_one * size_two)


def spectral_product(left_re, left_im, right_re, right_im, flipped):
    other_im = -right_im if flipped else right_im
    return (left_re * right_re - left_im * other_im, left_re * other_im + left_im * right_re)


def convolutions(inputs_chan, acts_chan, taps_chan):
    length = inputs_chan.shape[1]
    size_one, size_two = factor_pair(2 * length)
    padding = ((0, 0), (0, length))
    signal_re, signal_im = spectrum(jnp.pad(inputs_chan, padding), size_one, size_two)
    act_re, act_im = spectrum(jnp.pad(acts_chan, padding), size_one, size_two)
    taps_re, taps_im = spectrum(jnp.pad(taps_chan, padding), size_one, size_two)
    forward_re, forward_im = spectral_product(signal_re, signal_im, taps_re, taps_im, False)
    conv_chan = signal_of(forward_re, forward_im, size_one, size_two)[:, :length]
    back_re, back_im = spectral_product(act_re, act_im, taps_re, taps_im, True)
    back_chan = signal_of(back_re, back_im, size_one, size_two)[:, :length]
    cross_re, cross_im = spectral_product(act_re, act_im, signal_re, signal_im, True)
    taps_grad_chan = signal_of(cross_re, cross_im, size_one, size_two)[:, :length]
    return (conv_chan, back_chan, taps_grad_chan)


def on_device(activations, gate_values, output_grad, filter_codes, filter_scales):
    block_size = filter_codes.shape[0] // filter_scales.shape[0]
    scale_rows = jnp.repeat(filter_scales, block_size, axis=0)
    tokens_in = activations[0]
    gate_in = gate_values[0]
    grad_in = output_grad[0]
    grad_act = grad_in.astype(jnp.float32) * gate_in.astype(jnp.float32)
    inputs_chan, codes_chan = (
        lax.all_to_all(tokens_in.T, "seq", split_axis=0, concat_axis=1, tiled=True),
        lax.all_to_all(filter_codes.T, "seq", split_axis=0, concat_axis=1, tiled=True),
    )
    acts_chan, scales_chan = (
        lax.all_to_all(grad_act.T, "seq", split_axis=0, concat_axis=1, tiled=True),
        lax.all_to_all(filter_scales.T, "seq", split_axis=0, concat_axis=1, tiled=True),
    )
    taps_chan = codes_chan.astype(jnp.float32) * jnp.repeat(scales_chan, block_size, axis=1)
    conv_chan, back_chan, taps_grad_chan = convolutions(
        inputs_chan.astype(jnp.float32), acts_chan, taps_chan
    )
    conv_seq, back_seq, taps_grad_seq = (
        lax.all_to_all(conv_chan, "seq", split_axis=1, concat_axis=0, tiled=True),
        lax.all_to_all(back_chan, "seq", split_axis=1, concat_axis=0, tiled=True),
        lax.all_to_all(taps_grad_chan, "seq", split_axis=1, concat_axis=0, tiled=True),
    )
    gate_out = (grad_in.astype(jnp.float32) * conv_seq.T).astype(jnp.bfloat16)
    taps_total = lax.psum(taps_grad_seq.T, "dp")
    code_grad = taps_total * scale_rows
    return (back_seq.T[None], gate_out[None], code_grad)


def solution(mesh):
    in_specs = (
        P("dp", "seq", None),
        P("dp", "seq", None),
        P("dp", "seq", None),
        P("seq", None),
        P("seq", None),
    )
    out_specs = (P("dp", "seq", None), P("dp", "seq", None), P("seq", None))
    return jax.shard_map(
        on_device, mesh=mesh, in_specs=in_specs, out_specs=out_specs, check_vma=False
    )
```

profile of v0, /device:TPU:1, one launch (start us, length us, event | category | flops | bytes accessed | tf_op | source)
XLA Modules:
  0.0 375.7 jit_solution(14221738729266076005)
XLA Ops:
  9.3 10.0 %all-to-all-start.1 = ((bf16[32,8,1024]{2,1,0:T(8,128)(2,1)}), bf16[32,8,1024]{2,1,0:T(8,128)(2,1)S(1)}, u32[]{:S(2)}, u32[]{:S(2)}) async-start(bf16[32,8,1024]{2,1,0:T(8,128)(2,1)} %bitcast.13), calls=%async_computation.1 | async-start | bytes 1048576 | tf_op jit(solution)/shard_map/all_to_all | solution.py:91
  23.7 12.4 %all-to-all-done.1 = bf16[32,8,1024]{2,1,0:T(8,128)(2,1)S(1)} async-done(((bf16[32,8,1024]{2,1,0:T(8,128)(2,1)}), bf16[32,8,1024]{2,1,0:T(8,128)(2,1)S(1)}, u32[]{:S(2)}, u32[]{:S(2)}) %all-to-all-start.1) | async-done | bytes 524320 | tf_op jit(solution)/shard_map/all_to_all | solution.py:91
  36.2 3.7 all-to-all-start.2
  42.4 6.3 %all-to-all-done.2 = f32[32,8,8]{1,2,0:T(8,128)S(1)} async-done(((f32[32,8,8]{1,2,0:T(8,128)}), f32[32,8,8]{1,2,0:T(8,128)S(1)}, u32[]{:S(2)}, u32[]{:S(2)}) %all-to-all-start.2) | async-done | bytes 8224 | tf_op jit(solution)/shard_map/all_to_all | solution.py:95
  48.7 5.0 %all-to-all-start.4 = ((bf16[32,8,1024]{2,1,0:T(8,128)(2,1)}), bf16[32,8,1024]{2,1,0:T(8,128)(2,1)}, u32[]{:S(2)}, u32[]{:S(2)}) async-start(bf16[32,8,1024]{2,1,0:T(8,128)(2,1)} %bitcast.42), calls=%async_computation.4 | async-start | bytes 1048576 | tf_op jit(solution)/shard_map/all_to_all | solution.py:90
  54.1 3.3 fusion
  57.4 4.6 %fusion.2 = f32[256,8,256]{2,0,1:T(8,128)} fusion(f32[1,8,256,256]{3,1,2,0:T(8,128)S(1)} %bitcast.256), kind=kOutput, calls=%fused_computation.2 | convolution fusion | flops 1611530240 | bytes 4194304 | tf_op jit(solution)/shard_map/cab,ak->ckb/dot_general | solution.py:17
  62.0 8.4 %all-to-all-done.4 = bf16[32,8,1024]{2,1,0:T(8,128)(2,1)} async-done(((bf16[32,8,1024]{2,1,0:T(8,128)(2,1)}), bf16[32,8,1024]{2,1,0:T(8,128)(2,1)}, u32[]{:S(2)}, u32[]{:S(2)}) %all-to-all-start.4) | async-done | bytes 524320 | tf_op jit(solution)/shard_map/all_to_all | solution.py:90
  70.4 4.7 %all-to-all-start = ((f32[32,8,1024]{2,1,0:T(8,128)}), f32[32,8,1024]{2,1,0:T(8,128)}, u32[]{:S(2)}, u32[]{:S(2)}) async-start(f32[32,8,1024]{2,1,0:T(8,128)} %fusion.84), calls=%async_computation | async-start | bytes 2097152 | tf_op jit(solution)/shard_map/all_to_all | solution.py:94
  80.2 3.1 fusion.8
  83.3 3.1 fusion.10
  86.4 3.4 fusion.16
  89.8 3.0 fusion.18
  92.9 4.4 %fusion.81 = f32[8,256,256]{2,1,0:T(8,128)} fusion(f32[8,256,256]{2,1,0:T(8,128)S(1)} %fusion.8, f32[256,8,256]{2,0,1:T(8,128)S(1)} %fusion.88, f32[256,8,256]{2,0,1:T(8,128)S(1)} %fusion.86, f32[256,256]{1,0:T(8,128)S(1)} %copy.83, f32[256,256]{1,0:T(8,128)S(1)} %copy.82), kind=kOutput, calls=%fused_computation.80 | convolution fusion | flops 1613692928 | bytes 8912896 | tf_op jit(solution)/shard_map/ckb,bm->ckm/dot_general | solution.py:17
  97.2 4.4 %fusion.78 = f32[8,256,256]{2,1,0:T(8,128)} fusion(f32[8,256,256]{2,1,0:T(8,128)S(1)} %fusion.10, f32[256,8,256]{2,0,1:T(8,128)S(1)} %fusion.88, f32[256,8,256]{2,0,1:T(8,128)S(1)} %fusion.86, f32[256,256]{1,0:T(8,128)S(1)} %copy.83, f32[256,256]{1,0:T(8,128)S(1)} %copy.82), kind=kOutput, calls=%fused_computation.79 | convolution fusion | flops 1613627392 | bytes 8912896 | tf_op jit(solution)/shard_map/ckb,bm->ckm/dot_general | solution.py:17
  101.6 4.6 %fusion.75 = f32[8,256,256]{2,1,0:T(8,128)} fusion(f32[8,256,256]{2,1,0:T(8,128)S(1)} %fusion.16, f32[256,8,256]{2,0,1:T(8,128)S(1)} %fusion, f32[256,8,256]{2,0,1:T(8,128)S(1)} %copy-done, f32[256,256]{1,0:T(8,128)S(1)} %copy.83, f32[256,256]{1,0:T(8,128)S(1)} %copy.82), kind=kOutput, calls=%fused_computation.78 | convolution fusion | flops 1613692928 | bytes 8912896 | tf_op jit(solution)/shard_map/ckb,bm->ckm/dot_general | solution.py:17
  106.2 4.4 %fusion.72 = f32[8,256,256]{2,1,0:T(8,128)} fusion(f32[8,256,256]{2,1,0:T(8,128)S(1)} %fusion.18, f32[256,8,256]{2,0,1:T(8,128)S(1)} %fusion, f32[256,8,256]{2,0,1:T(8,128)S(1)} %copy-done, f32[256,256]{1,0:T(8,128)S(1)} %copy.83, f32[256,256]{1,0:T(8,128)S(1)} %copy.82), kind=kOutput, calls=%fused_computation.77 | convolution fusion | flops 1613627392 | bytes 8912896 | tf_op jit(solution)/shard_map/ckb,bm->ckm/dot_general | solution.py:17
  111.9 3.3 fusion.4
  115.3 3.3 fusion.6
  118.5 4.5 %fusion.24 = f32[8,256,256]{2,1,0:T(8,128)} fusion(f32[256,8,256]{2,0,1:T(8,128)S(1)} %fusion.4, f32[256,8,256]{2,0,1:T(8,128)S(1)} %fusion.6, f32[256,256]{1,0:T(8,128)S(1)} %copy.83, f32[256,256]{1,0:T(8,128)S(1)} %copy.82), kind=kOutput, calls=%fused_computation.24 | convolution fusion | flops 1613103104 | bytes 6815744 | tf_op jit(solution)/shard_map/ckb,bm->ckm/dot_general | solution.py:17
  123.1 3.0 fusion.26
  126.1 3.0 fusion.66
  129.5 8.9 %multiply_add_fusion = (f32[8,256,256]{2,1,0:T(8,128)S(1)}, f32[8,256,256]{2,1,0:T(8,128)S(1)}, f32[8,256,256]{2,1,0:T(8,128)}, f32[8,256,256]{2,1,0:T(8,128)}, ...) fusion(f32[8,256,256]{2,1,0:T(8,128)S(1)} %copy-done.5, f32[8,256,256]{2,1,0:T(8,128)S(1)} %fusion.66, ...), kind=kOutput, calls=%fused_computation.41 | convolution fusion | flops 1624178688 | bytes 29884416 | tf_op jit(solution)/shard_map/ckb,bm->ckm/dot_general | solution.py:17
  138.4 2.8 fusion.109
  141.2 2.8 fusion.131
  144.1 2.9 convolution_add_fusion
  147.0 2.9 convolution_subtract_fusion
  149.9 3.2 fusion.32
  153.1 3.2 multiply_bitcast_fusion
  158.6 8.0 %all-to-all-start.6 = ((f32[8,32,1024]{2,0,1:T(8,128)}), f32[8,32,1024]{2,0,1:T(8,128)}, u32[]{:S(2)}, u32[]{:S(2)}) async-start(f32[8,32,1024]{2,0,1:T(8,128)} %bitcast.265), calls=%async_computation.6 | async-start | bytes 2097152 | tf_op jit(solution)/shard_map/all_to_all | solution.py:104
  166.7 4.6 %fusion.112 = f32[8,256,256]{2,1,0:T(8,128)S(1)} fusion(f32[8,256,256]{2,1,0:T(8,128)} %get-tuple-element.15), kind=kOutput, calls=%fused_computation.124 | convolution fusion | flops 1611530240 | bytes 4194304 | tf_op jit(solution)/shard_map/ckm,mb->ckb/dot_general | solution.py:17
  171.3 2.9 fusion.134
  174.2 2.9 convolution_add_fusion.1
  177.0 2.9 convolution_subtract_fusion.1
  179.9 3.5 fusion.40
  183.5 3.3 multiply_bitcast_fusion.1
  189.0 5.4 %all-to-all-done.6 = f32[8,32,1024]{2,0,1:T(8,128)} async-done(((f32[8,32,1024]{2,0,1:T(8,128)}), f32[8,32,1024]{2,0,1:T(8,128)}, u32[]{:S(2)}, u32[]{:S(2)}) %all-to-all-start.6) | async-done | bytes 1048608 | tf_op jit(solution)/shard_map/all_to_all | solution.py:104
  194.4 4.7 %all-to-all-start.5 = ((f32[8,32,1024]{2,0,1:T(8,128)}), f32[8,32,1024]{2,0,1:T(8,128)}, u32[]{:S(2)}, u32[]{:S(2)}) async-start(f32[8,32,1024]{2,0,1:T(8,128)} %bitcast.263), calls=%async_computation.5 | async-start | bytes 2097152 | tf_op jit(solution)/shard_map/all_to_all | solution.py:102
  199.1 4.6 %fusion.118 = f32[8,256,256]{2,1,0:T(8,128)S(1)} fusion(f32[8,256,256]{2,1,0:T(8,128)} %get-tuple-element.17), kind=kOutput, calls=%fused_computation.130 | convolution fusion | flops 1611530240 | bytes 4194304 | tf_op jit(solution)/shard_map/ckm,mb->ckb/dot_general | solution.py:17
  203.7 2.8 fusion.139
  206.6 2.9 convolution_add_fusion.2
  209.4 2.9 convolution_subtract_fusion.2
  212.3 3.3 fusion.48
  215.7 3.3 multiply_bitcast_fusion.2
  221.2 5.8 %all-to-all-done.5 = f32[8,32,1024]{2,0,1:T(8,128)} async-done(((f32[8,32,1024]{2,0,1:T(8,128)}), f32[8,32,1024]{2,0,1:T(8,128)}, u32[]{:S(2)}, u32[]{:S(2)}) %all-to-all-start.5) | async-done | bytes 1048608 | tf_op jit(solution)/shard_map/all_to_all | solution.py:102
  227.0 3.9 %all-to-all-start.3 = ((f32[8,32,1024]{2,0,1:T(8,128)}), f32[8,32,1024]{2,0,1:T(8,128)S(1)}, u32[]{:S(2)}, u32[]{:S(2)}) async-start(f32[8,32,1024]{2,0,1:T(8,128)} %bitcast.34), calls=%async_computation.3 | async-start | bytes 2097152 | tf_op jit(solution)/shard_map/all_to_all | solution.py:103
  234.2 52.2 %all-to-all-done.3 = f32[8,32,1024]{2,0,1:T(8,128)S(1)} async-done(((f32[8,32,1024]{2,0,1:T(8,128)}), f32[8,32,1024]{2,0,1:T(8,128)S(1)}, u32[]{:S(2)}, u32[]{:S(2)}) %all-to-all-start.3) | async-done | bytes 1048608 | tf_op jit(solution)/shard_map/all_to_all | solution.py:103
  287.7 77.8 %all-reduce.5.cloned.1.call-done = f32[1024,256]{0,1:T(8,128)} async-done(((f32[1024,256]{0,1:T(8,128)}), f32[1024,256]{0,1:T(8,128)}) %all-reduce.5.cloned.1.call-update) | async-done | bytes 1048592 | tf_op jit(solution)/shard_map/psum | solution.py:107
  (60 shorter events, 30.8 us)
Async XLA Ops:
  7.2 12.2 %copy-start.11 = (f32[8,256]{1,0:T(8,128)S(1)}, f32[8,256]{1,0:T(8,128)}, u32[]{:S(2)}) copy-start(f32[8,256]{1,0:T(8,128)} %param.9) | copy-start | bytes 24580
  7.2 13.0 %copy-start.8 = (bf16[1,1024,256]{2,1,0:T(8,128)(2,1)S(1)}, bf16[1,1024,256]{2,1,0:T(8,128)(2,1)}, u32[]{:S(2)}) copy-start(bf16[1,1024,256]{2,1,0:T(8,128)(2,1)} %param.7) | copy-start | bytes 1572868
  7.2 13.2 %copy-start.9 = (bf16[1,1024,256]{2,1,0:T(8,128)(2,1)S(1)}, bf16[1,1024,256]{2,1,0:T(8,128)(2,1)}, u32[]{:S(2)}) copy-start(bf16[1,1024,256]{2,1,0:T(8,128)(2,1)} %param.6) | copy-start | bytes 1572868
  9.3 26.8 %all-to-all-start.1 = ((bf16[32,8,1024]{2,1,0:T(8,128)(2,1)}), bf16[32,8,1024]{2,1,0:T(8,128)(2,1)S(1)}, u32[]{:S(2)}, u32[]{:S(2)}) async-start(bf16[32,8,1024]{2,1,0:T(8,128)(2,1)} %bitcast.13), calls=%async_computation.1 | async-start | bytes 1048576 | tf_op jit(solution)/shard_map/all_to_all | solution.py:91
  22.6 18.7 %copy-start.10 = (bf16[1,1024,256]{2,1,0:T(8,128)(2,1)S(1)}, bf16[1,1024,256]{2,1,0:T(8,128)(2,1)}, u32[]{:S(2)}) copy-start(bf16[1,1024,256]{2,1,0:T(8,128)(2,1)} %param.5) | copy-start | bytes 1572868
  36.2 12.5 %all-to-all-start.2 = ((f32[32,8,8]{1,2,0:T(8,128)}), f32[32,8,8]{1,2,0:T(8,128)S(1)}, u32[]{:S(2)}, u32[]{:S(2)}) async-start(f32[32,8,8]{1,2,0:T(8,128)} %copy.87), calls=%async_computation.2 | async-start | bytes 262144 | tf_op jit(solution)/shard_map/all_to_all | solution.py:95
  48.7 21.7 %all-to-all-start.4 = ((bf16[32,8,1024]{2,1,0:T(8,128)(2,1)}), bf16[32,8,1024]{2,1,0:T(8,128)(2,1)}, u32[]{:S(2)}, u32[]{:S(2)}) async-start(bf16[32,8,1024]{2,1,0:T(8,128)(2,1)} %bitcast.42), calls=%async_computation.4 | async-start | bytes 1048576 | tf_op jit(solution)/shard_map/all_to_all | solution.py:90
  70.4 40.2 %all-to-all-start = ((f32[32,8,1024]{2,1,0:T(8,128)}), f32[32,8,1024]{2,1,0:T(8,128)}, u32[]{:S(2)}, u32[]{:S(2)}) async-start(f32[32,8,1024]{2,1,0:T(8,128)} %fusion.84), calls=%async_computation | async-start | bytes 2097152 | tf_op jit(solution)/shard_map/all_to_all | solution.py:94
  83.3 3.1 copy-start
  126.0 3.0 copy-start.4
  126.1 3.0 copy-start.5
  126.1 3.0 copy-start.6
  126.1 3.4 copy-start.7
  158.6 35.7 %all-to-all-start.6 = ((f32[8,32,1024]{2,0,1:T(8,128)}), f32[8,32,1024]{2,0,1:T(8,128)}, u32[]{:S(2)}, u32[]{:S(2)}) async-start(f32[8,32,1024]{2,0,1:T(8,128)} %bitcast.265), calls=%async_computation.6 | async-start | bytes 2097152 | tf_op jit(solution)/shard_map/all_to_all | solution.py:104
  166.7 4.6 %copy-start.3 = (f32[8,256,256]{2,1,0:T(8,128)S(1)}, f32[8,256,256]{2,1,0:T(8,128)}, u32[]{:S(2)}) copy-start(f32[8,256,256]{2,1,0:T(8,128)} %get-tuple-element.15) | copy-start | bytes 6291460
  171.3 2.9 copy-start.1
  194.4 32.6 %all-to-all-start.5 = ((f32[8,32,1024]{2,0,1:T(8,128)}), f32[8,32,1024]{2,0,1:T(8,128)}, u32[]{:S(2)}, u32[]{:S(2)}) async-start(f32[8,32,1024]{2,0,1:T(8,128)} %bitcast.263), calls=%async_computation.5 | async-start | bytes 2097152 | tf_op jit(solution)/shard_map/all_to_all | solution.py:102
  199.1 4.6 %copy-start.2 = (f32[8,256,256]{2,1,0:T(8,128)S(1)}, f32[8,256,256]{2,1,0:T(8,128)}, u32[]{:S(2)}) copy-start(f32[8,256,256]{2,1,0:T(8,128)} %get-tuple-element.17) | copy-start | bytes 6291460
  227.0 59.4 %all-to-all-start.3 = ((f32[8,32,1024]{2,0,1:T(8,128)}), f32[8,32,1024]{2,0,1:T(8,128)S(1)}, u32[]{:S(2)}, u32[]{:S(2)}) async-start(f32[8,32,1024]{2,0,1:T(8,128)} %bitcast.34), calls=%async_computation.3 | async-start | bytes 2097152 | tf_op jit(solution)/shard_map/all_to_all | solution.py:103
  230.9 134.6 %all-reduce.5.cloned.1.call-start = ((), (), s32[]{:S(2)}) async-start(), calls=%async_computation.7 | async-start | bytes 2097152 | tf_op jit(solution)/shard_map/psum | solution.py:107
Sparse Core Ops, SparseCore 0:
  234.4 131.0 all-reduce.4
where the time goes:
time: 381 us; the launch traced here: 376 us
  waiting for transfers between devices  169 us (44%)
  matrix products  126 us (33%)
  starting transfers between devices  40.1 us (11%)
  local copies, waits for them, and re-layouts  18.7 us (5%)
  between operations  14.9 us (4%)
  other arithmetic  7.41 us (2%)
    dot_general x36, matrix products, contract(): return jnp.einsum(pattern, left, right, precision=lax.Precision.HIGHEST)  126 us
    psum x1, waiting for transfers between devices, on_device(): taps_total = lax.psum(taps_grad_seq.T, 'dp')  77.8 us
    all_to_all x1, waiting for transfers between devices, on_device(): lax.all_to_all(back_chan, 'seq', split_axis=1, concat_axis=0, tiled=True)  52.2 us
    all_to_all x1, waiting for transfers between devices, on_device(): lax.all_to_all(filter_codes.T, 'seq', split_axis=0, concat_axis=1, tiled=...  12.4 us
    unnamed x35, local copies, waits for them, and re-layouts  11.4 us
    all_to_all x1, starting transfers between devices, on_device(): lax.all_to_all(filter_codes.T, 'seq', split_axis=0, concat_axis=1, tiled=...  10 us
    all_to_all x1, waiting for transfers between devices, on_device(): lax.all_to_all(tokens_in.T, 'seq', split_axis=0, concat_axis=1, tiled=True)  8.36 us
    all_to_all x1, starting transfers between devices, on_device(): lax.all_to_all(taps_grad_chan, 'seq', split_axis=1, concat_axis=0, tiled=...  8.04 us
  transfers between devices with their start and end apart: 8, of which 7 were waited for; matrix products, arithmetic and copies ran while one was open for 26% of the time, Pallas kernels for 0%

commit v1 on v0

v1 whole, which is shorter than its diff:
```python
import math

import jax
import jax.numpy as jnp
import numpy as np
from jax import lax
from jax.experimental import pallas as pl
from jax.experimental.pallas import tpu as pltpu
from jax.sharding import PartitionSpec as P

BOTH = ("seq", "dp")
LANES = 128
SUB = 8
ROWS = 256
FLOOR = 2.0**-90
TOP8 = 2.0**15
TOP16 = 2.0**7.5


def split_np(table):
    high = np.asarray(table, np.float64).astype(jnp.bfloat16)
    low = (np.asarray(table, np.float64) - high.astype(np.float64)).astype(jnp.bfloat16)
    return high, low


def tables():
    whole = 2 * ROWS * LANES
    rows = np.arange(ROWS, dtype=np.float64)
    lanes = np.arange(LANES, dtype=np.float64)
    outer = 2 * np.pi * (rows[:, None] + 0.5) * rows[None, :] / (2 * ROWS)
    first = np.concatenate([np.cos(outer), -np.sin(outer)], axis=0)
    last = np.concatenate([np.cos(outer.T), -np.sin(outer.T)], axis=1) * (2.0 / whole)
    inner = 2 * np.pi * lanes[:, None] * lanes[None, :] / LANES
    cos, sin = np.cos(inner), np.sin(inner)
    forward = np.block([[cos, -sin], [sin, cos]])
    backward = np.block([[cos, sin], [-sin, cos]])
    turn = 2 * np.pi * (rows[:, None] + 0.5) * lanes[None, :] / whole
    twist = np.stack([np.cos(turn), -np.sin(turn)]).astype(np.float32)
    first_hi, first_lo = split_np(first)
    last_hi, last_lo = split_np(last)
    return (
        np.concatenate([first_hi, first_lo], axis=0),
        np.concatenate([last_hi, last_lo], axis=0),
        np.stack(split_np(forward)),
        np.stack(split_np(backward)),
        twist,
    )


def dot(left, right):
    return jnp.dot(left, right, preferred_element_type=jnp.float32)


def halves(value):
    high = value.astype(jnp.bfloat16)
    low = (value - high.astype(jnp.float32)).astype(jnp.bfloat16)
    return high, low


def left_product(table_ref, high, low):
    count = table_ref.shape[0] // 2
    both = dot(table_ref[...], high)
    total = both[:count] + both[count:]
    if low is not None:
        total = total + dot(table_ref[:count], low)
    return total


def right_product(value, table_ref):
    high, low = halves(value)
    return dot(high, table_ref[0]) + dot(low, table_ref[0]) + dot(high, table_ref[1])


def forward(high, low, first_ref, forward_ref, twist_ref):
    section = left_product(first_ref, high, low)
    cos, sin = twist_ref[0], twist_ref[1]
    out = []
    for start in range(0, high.shape[1], LANES):
        real = section[:ROWS, start : start + LANES]
        imag = section[ROWS:, start : start + LANES]
        turned = jnp.concatenate([real * cos - imag * sin, real * sin + imag * cos], axis=1)
        out.append(right_product(turned, forward_ref))
    return out


def inverse(spectra, last_ref, backward_ref, twist_ref):
    cos, sin = twist_ref[0], twist_ref[1]
    sections = []
    for spec in spectra:
        part = right_product(spec, backward_ref)
        real, imag = part[:, :LANES], part[:, LANES:]
        sections.append(jnp.concatenate([real * cos + imag * sin, imag * cos - real * sin], axis=0))
    high, low = halves(jnp.concatenate(sections, axis=1))
    result = left_product(last_ref, high, low)
    return [result[:, i * LANES : (i + 1) * LANES] for i in range(len(spectra))]


def times(left, right):
    lr, li, rr, ri = left[:, :LANES], left[:, LANES:], right[:, :LANES], right[:, LANES:]
    return jnp.concatenate([lr * rr - li * ri, lr * ri + li * rr], axis=1)


def times_conj(left, right):
    lr, li, rr, ri = left[:, :LANES], left[:, LANES:], right[:, :LANES], right[:, LANES:]
    return jnp.concatenate([lr * rr + li * ri, li * rr - lr * ri], axis=1)


def eighth_power(value):
    two = value * value
    four = two * two
    return four * two * value * jnp.abs(value)


def sixteenth_power(value):
    two = value * value
    four = two * two
    return four * four * four * two * value * jnp.abs(value)


def root_of(code, steps):
    size = jnp.exp2(jnp.log2(jnp.abs(code)) * (1.0 / 2**steps))
    return jnp.where(code < 0, -size, size)


def transform_kernel(scale_ref, data_ref, taps_ref, first_ref, last_ref, forward_ref, backward_ref, twist_ref,
                     out_ref, out_scale_ref, grad_ref):
    segments, replicas = data_ref.shape[0], data_ref.shape[1]
    taps_high, taps_low = halves(taps_ref[...])
    (taps_spec,) = forward(taps_high, taps_low, first_ref, forward_ref, twist_ref)

    def pair(step, cross):
        signals, acts = [], []
        for half in range(2):
            index = step * 2 + half
            tile = data_ref[:, index].astype(jnp.float32)
            signals.append(tile[:, :SUB].reshape(ROWS, LANES).astype(jnp.bfloat16))
            rooted = root_of(tile[:, SUB:], 3)
            parts = [rooted[s] * scale_ref[s * replicas + index] for s in range(segments)]
            acts.append(jnp.concatenate(parts, axis=0))
        act_high, act_low = halves(jnp.concatenate(acts, axis=1))
        signal_specs = forward(jnp.concatenate(signals, axis=1), None, first_ref, forward_ref, twist_ref)
        act_specs = forward(act_high, act_low, first_ref, forward_ref, twist_ref)
        for signal_spec, act_spec in zip(signal_specs, act_specs):
            cross = cross + times_conj(act_spec, signal_spec)
        convs = inverse([times(s, taps_spec) for s in signal_specs], last_ref, backward_ref, twist_ref)
        backs = inverse([times_conj(a, taps_spec) for a in act_specs], last_ref, backward_ref, twist_ref)
        for half in range(2):
            index = step * 2 + half
            conv, back = convs[half], backs[half]
            conv_top = jnp.maximum(jnp.max(jnp.abs(conv), keepdims=True), FLOOR)
            back_top = jnp.maximum(jnp.max(jnp.abs(back), keepdims=True), FLOOR)
            conv_code = sixteenth_power(conv * (TOP16 / conv_top)).reshape(segments, SUB, LANES)
            back_code = eighth_power(back * (TOP8 / back_top)).reshape(segments, SUB, LANES)
            out_ref[:, index] = jnp.concatenate([conv_code, back_code], axis=1).astype(jnp.bfloat16)
            out_scale_ref[index] = jnp.concatenate(
                [jnp.broadcast_to(conv_top * (1.0 / TOP16), (1, LANES)), jnp.broadcast_to(back_top * (1.0 / TOP8), (1, LANES))],
                axis=0,
            )
        return cross

    cross = lax.fori_loop(0, replicas // 2, pair, jnp.zeros((ROWS, 2 * LANES), jnp.float32))
    (grad,) = inverse([cross], last_ref, backward_ref, twist_ref)
    grad_ref[...] = grad


def transforms(scales, data, taps):
    segments, replicas = data.shape[0], data.shape[1]
    vmem = pl.BlockSpec(memory_space=pltpu.VMEM)
    return pl.pallas_call(
        transform_kernel,
        out_shape=(
            jax.ShapeDtypeStruct(data.shape, jnp.bfloat16),
            jax.ShapeDtypeStruct((replicas, 2, LANES), jnp.float32),
            jax.ShapeDtypeStruct((ROWS, LANES), jnp.float32),
        ),
        in_specs=[pl.BlockSpec(memory_space=pltpu.SMEM)] + [vmem] * 7,
        out_specs=(vmem, vmem, vmem),
        compiler_params=pltpu.CompilerParams(vmem_limit_bytes=48 << 20),
        cost_estimate=pl.CostEstimate(flops=7_000_000_000, bytes_accessed=5_000_000, transcendentals=500_000),
    )(scales, data, taps, *[jnp.asarray(t) for t in tables()])


def by_channel(value):
    return value.reshape(SUB, LANES, value.shape[-1]).transpose(2, 0, 1)


def by_position(value):
    return value.transpose(1, 2, 0).reshape(SUB * LANES, value.shape[0])


def on_device(activations, gate_values, output_grad, filter_codes, filter_scales):
    channels = filter_codes.shape[1]
    seqs, replicas = lax.axis_size("seq"), lax.axis_size("dp")
    replica = lax.axis_index("dp")
    block_size = filter_codes.shape[0] // filter_scales.shape[0]
    grad_in = output_grad[0].astype(jnp.float32)
    act = grad_in * gate_values[0].astype(jnp.float32)
    top = jnp.maximum(jnp.max(jnp.abs(act)), FLOOR)
    scale_all = lax.all_gather((top * (1.0 / TOP8)).reshape(1), BOTH, tiled=True)
    act_code = eighth_power(act * (TOP8 / top)).astype(jnp.bfloat16)
    sent = jnp.concatenate([by_channel(activations[0]), by_channel(act_code)], axis=1)
    got = lax.all_to_all(sent, BOTH, 0, 0, tiled=True)

    scale_rows = jnp.repeat(filter_scales, block_size, axis=0)
    taps = by_channel(filter_codes.astype(jnp.float32) * scale_rows)
    taps_mine = lax.dynamic_index_in_dim(taps.reshape(seqs, replicas, SUB, LANES), replica, 1, keepdims=False)
    taps_got = lax.all_to_all(taps_mine, "seq", 0, 0, tiled=True)

    out, out_scale, grad = transforms(
        scale_all, got.reshape(seqs, replicas, 2 * SUB, LANES), taps_got.reshape(ROWS, LANES)
    )
    out_scale_all = lax.all_gather(out_scale[:, :, 0], BOTH)
    back = lax.all_to_all(out.reshape(channels, 2 * SUB, LANES), BOTH, 0, 0, tiled=True)
    grad_seq = lax.all_to_all(grad.reshape(seqs, SUB, LANES), "seq", 0, 0, tiled=True)
    grad_all = lax.all_gather(grad_seq, "dp", axis=1).reshape(channels, SUB, LANES)

    my_scale = lax.dynamic_index_in_dim(out_scale_all, replica, 1, keepdims=False)
    back = back.astype(jnp.float32)
    conv = by_position(root_of(back[:, :SUB], 4) * my_scale[:, 0, None, None])
    input_grad = by_position(root_of(back[:, SUB:], 3) * my_scale[:, 1, None, None])
    gate_grad = (grad_in * conv).astype(jnp.bfloat16)
    code_grad = by_position(grad_all) * scale_rows
    return (input_grad[None], gate_grad[None], code_grad)


def solution(mesh):
    in_specs = (
        P("dp", "seq", None),
        P("dp", "seq", None),
        P("dp", "seq", None),
        P("seq", None),
        P("seq", None),
    )
    out_specs = (P("dp", "seq", None), P("dp", "seq", None), P("seq", None))
    return jax.shard_map(on_device, mesh=mesh, in_specs=in_specs, out_specs=out_specs, check_vma=False)
```

time: 381 us -> 860 us (2.26)
  blocking collectives: 0 us -> 784 us
  waiting for transfers between devices: 169 us -> 5.22 us
  matrix products: 126 us -> 0 us
  Pallas kernels: 0 us -> 14.2 us
  starting transfers between devices: 40.1 us -> 26.8 us
  local copies, waits for them, and re-layouts: 18.7 us -> 7.32 us
    all_gather x0 -> x1, blocking collectives: none -> 689 us  [on_device(): out_scale_all = lax.all_gather(out_scale[:, :, 0], BOTH)]
    dot_general x36 -> x0, matrix products: 126 us -> none  [contract(): return jnp.einsum(pattern, left, right, precision=lax.Precision.HIGHEST)]
    all_to_all x7 -> x3, waiting for transfers between devices: 90.4 us -> 4.54 us  [the longest x1 4.54 us: on_device(): taps_got = lax.all_to_all(taps_mine, 'seq', 0, 0, tiled=True)]
    unnamed x0 -> x1, blocking collectives: none -> 79.9 us
    psum x1 -> x0, waiting for transfers between devices: 77.8 us -> none  [on_device(): taps_total = lax.psum(taps_grad_seq.T, 'dp')]
    all_to_all x0 -> x1, blocking collectives: none -> 14.3 us  [on_device(): lax.all_to_all(grad.reshape(seqs, SUB, LANES), 'seq', 0, 0, tiled=True)]
    pallas_call x0 -> x1, Pallas kernels: none -> 14.2 us  [transforms(): pl.pallas_call(transform_kernel, out_shape=(jax.ShapeDtypeStruct(data.sha...]
    all_to_all x7 -> x3, starting transfers between devices: 40 us -> 26.7 us  [the longest x1 10.2 us: on_device(): got = lax.all_to_all(sent, BOTH, 0, 0, tiled=True)]
  transfers between devices with their start and end apart: 8 -> 4, of which waited for: 7 -> 1; matrix products, arithmetic and copies ran while one was open for 26% -> 1% of each run, Pallas kernels for 0% -> 0%
where the time goes in v1:
time: 860 us
  blocking collectives  784 us (91%)
  starting transfers between devices  26.8 us (3%)
  between operations  15 us (2%)
  Pallas kernels  14.2 us (2%)
    all_gather x1, blocking collectives, on_device(): out_scale_all = lax.all_gather(out_scale[:, :, 0], BOTH)  689 us
    unnamed x1, blocking collectives  79.9 us
  transfers between devices with their start and end apart: 4, of which 1 were waited for; matrix products, arithmetic and copies ran while one was open for 1% of the time, Pallas kernels for 0%

profile of v1, /device:TPU:1, one launch (start us, length us, event | category | flops | bytes accessed | tf_op | source)
XLA Modules:
  0.0 859.6 jit_solution(16145754355770370721)
XLA Ops:
  7.2 0.0 copy-start.5
  7.2 0.0 copy-start.6
  7.2 1.2 bitcast_multiply_fusion.1
  8.4 0.4 copy.53
  8.8 0.7 dynamic-slice_bitcast_fusion
  9.5 10.0 %all-to-all-start.1 = ((f32[32,8,128]{2,1,0:T(8,128)}), f32[32,8,128]{2,1,0:T(8,128)S(1)}, u32[]{:S(2)}, u32[]{:S(2)}) async-start(f32[32,8,128]{2,1,0:T(8,128)} %dynamic-slice_bitcast_fusion), calls=%async_computation.1 | async-start | bytes 262144 | tf_op jit(solution)/shard_map/all_to_all | solution.py:207
  19.5 0.0 copy-done.5
  19.5 0.0 copy-done.6
  19.5 0.7 abs_reduce_fusion
  21.0 0.1 fusion.8
  21.1 0.0 copy-start.7
  21.1 0.4 copy.43
  21.5 0.2 fusion.9
  21.8 0.4 copy-done.7
  22.2 0.3 copy.42
  22.5 0.0 copy-start
  22.5 0.0 copy-start.1
  22.5 0.0 copy-start.2
  22.5 0.0 copy-start.3
  22.5 0.0 copy-start.4
  22.5 1.2 pad_maximum_fusion
  23.7 4.5 all-to-all-done.1
  28.2 10.2 %all-to-all-start = ((bf16[256,16,128]{2,1,0:T(8,128)(2,1)}), bf16[256,16,128]{2,1,0:T(8,128)(2,1)S(1)}, u32[]{:S(2)}, u32[]{:S(2)}) async-start(bf16[256,16,128]{2,1,0:T(8,128)(2,1)} %pad_maximum_fusion), calls=%async_computation | async-start | bytes 2097152 | tf_op jit(solution)/shard_map/all_to_all | solution.py:202
  38.4 0.1 dynamic-update-slice
  38.6 79.9 %all-reduce.scale_ref = f32[256]{0:T(256)S(1)} all-reduce(f32[256]{0:T(256)S(1)} %dynamic-update-slice), channel_id=1, replica_groups=mesh['seq'=32,'dp'=8] {'seq','dp'}, use_global_device_ids=true, to_apply=%add | all-reduce | flops 256 | bytes 2048
  118.5 0.0 all-to-all-done
  118.5 0.0 copy-done
  118.5 0.0 copy-done.1
  118.5 0.0 copy-done.2
  118.5 14.2 %shard_map.121 = (bf16[32,8,16,128]{3,2,1,0:T(8,128)(2,1)}, f32[8,2,128]{2,1,0:T(2,128)S(1)}, f32[256,128]{1,0:T(8,128)S(1)}) custom-call(f32[256]{0:T(256)S(1)} %all-reduce.scale_ref, bf16[32,8,16,128]{3,2,1,0:T(8,128)(2,1)S(1)} %bitcast.37, f32[256,128]{1,0:T(8,128)S(1)} %bitcast.38, bf16[1024,256]{1,0:T(8,128)(2,1)S(1)} %copy-done, ...), custom_call_target="tpu_custom_call" | custom-call | flops 7000000000 | bytes 5000000 | tf_op jit(solution)/shard_map/pallas_call | solution.py:169
  132.6 14.3 %all_to_all.20 = f32[32,8,128]{2,1,0:T(8,128)} all-to-all(f32[32,8,128]{2,1,0:T(8,128)S(1)} %bitcast.39), channel_id=1, replica_groups=mesh['seq'=32,'dp'=8] {'seq'}, dimensions={0} | all-to-all | bytes 262144 | tf_op jit(solution)/shard_map/all_to_all | solution.py:214
  147.0 6.5 all-to-all-start.2
  153.5 0.0 all-gather.4.cloned.1.call-start
  153.6 0.7 all-gather.4.cloned.1.call-update
  154.2 0.1 copy.48
  154.4 689.5 %all-gather = f32[2048,2,1]{1,2,0:T(1,128)S(1)} all-gather(f32[8,2,1]{1,2,0:T(1,128)S(1)} %copy.48), channel_id=2, replica_groups=mesh['seq'=32,'dp'=8] {'seq','dp'}, dimensions={0}, use_global_device_ids=true | all-gather | bytes 16448 | tf_op jit(solution)/shard_map/all_gather | solution.py:212
  843.9 0.1 constant_dynamic-slice_fusion
  844.0 0.1 fusion.10
  844.1 0.1 copy.57
  844.1 0.1 copy.58
  844.2 0.0 all-to-all-done.2
  844.2 0.2 convert_element_type.31
  844.4 1.9 fusion.7
  846.3 1.6 copy.51
  847.9 1.4 copy.50
  849.2 0.9 fusion
  850.2 1.6 copy.52
  851.7 1.1 bitcast_multiply_fusion
  (6 shorter events, 0.0 us)
Async XLA Ops:
  7.2 12.3 %copy-start.5 = (bf16[1,1024,256]{2,1,0:T(8,128)(2,1)S(1)}, bf16[1,1024,256]{2,1,0:T(8,128)(2,1)}, u32[]{:S(2)}) copy-start(bf16[1,1024,256]{2,1,0:T(8,128)(2,1)} %param.12) | copy-start | bytes 1572868
  7.2 12.3 %copy-start.6 = (bf16[1,1024,256]{2,1,0:T(8,128)(2,1)S(1)}, bf16[1,1024,256]{2,1,0:T(8,128)(2,1)}, u32[]{:S(2)}) copy-start(bf16[1,1024,256]{2,1,0:T(8,128)(2,1)} %param.11) | copy-start | bytes 1572868
  9.5 18.7 %all-to-all-start.1 = ((f32[32,8,128]{2,1,0:T(8,128)}), f32[32,8,128]{2,1,0:T(8,128)S(1)}, u32[]{:S(2)}, u32[]{:S(2)}) async-start(f32[32,8,128]{2,1,0:T(8,128)} %dynamic-slice_bitcast_fusion), calls=%async_computation.1 | async-start | bytes 262144 | tf_op jit(solution)/shard_map/all_to_all | solution.py:207
  21.1 1.0 copy-start.7
  22.5 96.0 %copy-start = (bf16[1024,256]{1,0:T(8,128)(2,1)S(1)}, bf16[1024,256]{1,0:T(8,128)(2,1)}, u32[]{:S(2)}) copy-start(bf16[1024,256]{1,0:T(8,128)(2,1)} %constant.44.clone.first_ref) | copy-start | bytes 1572868
  22.5 96.0 %copy-start.1 = (bf16[512,512]{1,0:T(8,128)(2,1)S(1)}, bf16[512,512]{1,0:T(8,128)(2,1)}, u32[]{:S(2)}) copy-start(bf16[512,512]{1,0:T(8,128)(2,1)} %constant.45.clone.last_ref) | copy-start | bytes 1572868
  22.5 96.0 %copy-start.2 = (bf16[2,256,256]{2,1,0:T(8,128)(2,1)S(1)}, bf16[2,256,256]{2,1,0:T(8,128)(2,1)}, u32[]{:S(2)}) copy-start(bf16[2,256,256]{2,1,0:T(8,128)(2,1)} %constant.46.clone.forward_ref) | copy-start | bytes 786436
  22.5 96.0 %copy-start.3 = (bf16[2,256,256]{2,1,0:T(8,128)(2,1)S(1)}, bf16[2,256,256]{2,1,0:T(8,128)(2,1)}, u32[]{:S(2)}) copy-start(bf16[2,256,256]{2,1,0:T(8,128)(2,1)} %constant.47.clone.backward_ref) | copy-start | bytes 786436
  22.5 96.0 %copy-start.4 = (f32[2,256,128]{2,1,0:T(8,128)S(1)}, f32[2,256,128]{2,1,0:T(8,128)}, u32[]{:S(2)}) copy-start(f32[2,256,128]{2,1,0:T(8,128)} %constant.48.clone.twist_ref) | copy-start | bytes 786436
  28.2 90.2 %all-to-all-start = ((bf16[256,16,128]{2,1,0:T(8,128)(2,1)}), bf16[256,16,128]{2,1,0:T(8,128)(2,1)S(1)}, u32[]{:S(2)}, u32[]{:S(2)}) async-start(bf16[256,16,128]{2,1,0:T(8,128)(2,1)} %pad_maximum_fusion), calls=%async_computation | async-start | bytes 2097152 | tf_op jit(solution)/shard_map/all_to_all | solution.py:202
  147.0 697.3 %all-to-all-start.2 = ((bf16[256,16,128]{2,1,0:T(8,128)(2,1)}), bf16[256,16,128]{2,1,0:T(8,128)(2,1)S(1)}, u32[]{:S(2)}, u32[]{:S(2)}) async-start(bf16[256,16,128]{2,1,0:T(8,128)(2,1)} %bitcast.12), calls=%async_computation.2 | async-start | bytes 2097152 | tf_op jit(solution)/shard_map/all_to_all | solution.py:213
  153.5 696.7 %all-gather.4.cloned.1.call-start = ((), (), s32[]{:S(2)}) async-start(), calls=%async_computation.4 | async-start | bytes 1179648 | tf_op jit(solution)/shard_map/all_gather | solution.py:215
  849.2 2.5 copy-start.8
Sparse Core Ops, SparseCore 0:
  156.8 63.5 all-gather.3

commit v2 on v1

--- a/solution.py
+++ b/solution.py
@@ -1,4 +1,4 @@
-import math
+import functools
 
 import jax
 import jax.numpy as jnp
@@ -8,13 +8,13 @@
 from jax.experimental.pallas import tpu as pltpu
 from jax.sharding import PartitionSpec as P
 
-BOTH = ("seq", "dp")
 LANES = 128
 SUB = 8
 ROWS = 256
 FLOOR = 2.0**-90
 TOP8 = 2.0**15
 TOP16 = 2.0**7.5
+STRIDE = 37
 
 
 def split_np(table):
@@ -123,7 +123,7 @@
 
 
 def transform_kernel(scale_ref, data_ref, taps_ref, first_ref, last_ref, forward_ref, backward_ref, twist_ref,
-                     out_ref, out_scale_ref, grad_ref):
+                     out_ref, grad_ref):
     segments, replicas = data_ref.shape[0], data_ref.shape[1]
     taps_high, taps_low = halves(taps_ref[...])
     (taps_spec,) = forward(taps_high, taps_low, first_ref, forward_ref, twist_ref)
@@ -135,7 +135,7 @@
             tile = data_ref[:, index].astype(jnp.float32)
             signals.append(tile[:, :SUB].reshape(ROWS, LANES).astype(jnp.bfloat16))
             rooted = root_of(tile[:, SUB:], 3)
-            parts = [rooted[s] * scale_ref[s * replicas + index] for s in range(segments)]
+            parts = [rooted[s] * scale_ref[s, pl.ds(index, 1)] for s in range(segments)]
             acts.append(jnp.concatenate(parts, axis=0))
         act_high, act_low = halves(jnp.concatenate(acts, axis=1))
         signal_specs = forward(jnp.concatenate(signals, axis=1), None, first_ref, forward_ref, twist_ref)
@@ -152,15 +152,15 @@
             conv_code = sixteenth_power(conv * (TOP16 / conv_top)).reshape(segments, SUB, LANES)
             back_code = eighth_power(back * (TOP8 / back_top)).reshape(segments, SUB, LANES)
             out_ref[:, index] = jnp.concatenate([conv_code, back_code], axis=1).astype(jnp.bfloat16)
-            out_scale_ref[index] = jnp.concatenate(
-                [jnp.broadcast_to(conv_top * (1.0 / TOP16), (1, LANES)), jnp.broadcast_to(back_top * (1.0 / TOP8), (1, LANES))],
-                axis=0,
-            )
+            lane = lax.broadcasted_iota(jnp.int32, (1, LANES), 1)
+            row = jnp.where(lane < LANES // 2, conv_top * (1.0 / TOP16), back_top * (1.0 / TOP8))
+            for s in range(segments):
+                grad_ref[s, pl.ds(SUB + index, 1)] = row
         return cross
 
     cross = lax.fori_loop(0, replicas // 2, pair, jnp.zeros((ROWS, 2 * LANES), jnp.float32))
     (grad,) = inverse([cross], last_ref, backward_ref, twist_ref)
-    grad_ref[...] = grad
+    grad_ref[:, :SUB] = grad.reshape(segments, SUB, LANES)
 
 
 def transforms(scales, data, taps):
@@ -170,16 +170,191 @@
         transform_kernel,
         out_shape=(
             jax.ShapeDtypeStruct(data.shape, jnp.bfloat16),
-            jax.ShapeDtypeStruct((replicas, 2, LANES), jnp.float32),
-            jax.ShapeDtypeStruct((ROWS, LANES), jnp.float32),
+            jax.ShapeDtypeStruct((segments, SUB + replicas, LANES), jnp.float32),
         ),
-        in_specs=[pl.BlockSpec(memory_space=pltpu.SMEM)] + [vmem] * 7,
-        out_specs=(vmem, vmem, vmem),
+        in_specs=[vmem] * 8,
+        out_specs=(vmem, vmem),
         compiler_params=pltpu.CompilerParams(vmem_limit_bytes=48 << 20),
         cost_estimate=pl.CostEstimate(flops=7_000_000_000, bytes_accessed=5_000_000, transcendentals=500_000),
     )(scales, data, taps, *[jnp.asarray(t) for t in tables()])
 
 
+def to_peer(source, target, sems, row, seq, dp):
+    return pltpu.make_async_remote_copy(
+        src_ref=source, dst_ref=target, send_sem=sems.at[0, row], recv_sem=sems.at[1, row],
+        device_id={"seq": seq, "dp": dp}, device_id_type=pl.DeviceIdType.MESH,
+    )
+
+
+def greet(seqs, dps, seq, dp):
+    barrier = pltpu.get_barrier_semaphore()
+    count = seqs * dps
+    mine = seq * dps + dp
+
+    def signal(offset, carry):
+        peer = lax.rem(mine + offset, count)
+        pl.semaphore_signal(
+            barrier, inc=1, device_id={"seq": peer // dps, "dp": lax.rem(peer, dps)}, device_id_type=pl.DeviceIdType.MESH
+        )
+        return carry
+
+    lax.fori_loop(1, count, signal, 0)
+    pl.semaphore_wait(barrier, count - 1)
+
+
+def send_all(seqs, dps, seq, dp, source_ref, target_ref, sems, row):
+    count = seqs * dps
+    mine = seq * dps + dp
+
+    def send(offset, carry):
+        peer = lax.rem(mine + offset * STRIDE, count)
+        to_peer(source_ref.at[peer], target_ref.at[mine], sems, row, peer // dps, lax.rem(peer, dps)).start()
+        return carry
+
+    lax.fori_loop(1, count, send, 0)
+
+
+def gather_kernel(seqs, dps, data_ref, taps_ref, scale_ref, got_ref, taps_got_ref, scales_got_ref,
+                  dp_scale, scale_tile, sems, local_sems):
+    seq, dp = lax.axis_index("seq"), lax.axis_index("dp")
+    mine = seq * dps + dp
+    greet(seqs, dps, seq, dp)
+
+    def send_scale(offset, carry):
+        to_peer(scale_ref, dp_scale.at[dp], sems, 0, seq, lax.rem(dp + offset, dps)).start()
+        return carry
+
+    lax.fori_loop(1, dps, send_scale, 0)
+    send_all(seqs, dps, seq, dp, data_ref, got_ref, sems, 1)
+
+    def send_taps(offset, carry):
+        peer = lax.rem(seq + offset, seqs)
+        to_peer(taps_ref.at[peer, dp], taps_got_ref.at[seq], sems, 2, peer, dp).start()
+        return carry
+
+    lax.fori_loop(1, seqs, send_taps, 0)
+    own = pltpu.make_async_copy(data_ref.at[mine], got_ref.at[mine], local_sems.at[0])
+    own.start()
+    own_taps = pltpu.make_async_copy(taps_ref.at[seq, dp], taps_got_ref.at[seq], local_sems.at[1])
+    own_taps.start()
+
+    next_dp, next_seq = lax.rem(dp + 1, dps), lax.rem(seq + 1, seqs)
+    to_peer(dp_scale.at[pl.ds(0, dps - 1)], dp_scale.at[pl.ds(0, dps - 1)], sems, 0, seq, next_dp).wait()
+    own.wait()
+    own_taps.wait()
+    dp_scale[dp] = scale_ref[...]
+    for other in range(dps):
+        scale_tile[other : other + 1] = dp_scale[other, 0:1]
+
+    def send_tile(offset, carry):
+        to_peer(scale_tile, scales_got_ref.at[seq], sems, 3, lax.rem(seq + offset, seqs), dp).start()
+        return carry
+
+    lax.fori_loop(1, seqs, send_tile, 0)
+    rest = pl.ds(0, seqs - 1)
+    to_peer(taps_got_ref.at[rest], taps_got_ref.at[rest], sems, 2, next_seq, dp).wait()
+    rest_all = pl.ds(0, seqs * dps - 1)
+    to_peer(got_ref.at[rest_all], got_ref.at[rest_all], sems, 1, next_seq, dp).wait()
+    to_peer(scales_got_ref.at[rest], scales_got_ref.at[rest], sems, 3, next_seq, dp).wait()
+    scales_got_ref[seq] = scale_tile[...]
+
+
+def gather(data, taps, scale):
+    seqs, dps = taps.shape[0], taps.shape[1]
+    vmem = pl.BlockSpec(memory_space=pltpu.VMEM)
+    return pl.pallas_call(
+        functools.partial(gather_kernel, seqs, dps),
+        out_shape=(
+            jax.ShapeDtypeStruct(data.shape, data.dtype),
+            jax.ShapeDtypeStruct((seqs, SUB, LANES), jnp.float32),
+            jax.ShapeDtypeStruct((seqs, SUB, LANES), jnp.float32),
+        ),
+        in_specs=[vmem] * 3,
+        out_specs=(vmem,) * 3,
+        scratch_shapes=[
+            pltpu.VMEM((dps, SUB, LANES), jnp.float32),
+            pltpu.VMEM((SUB, LANES), jnp.float32),
+            pltpu.SemaphoreType.DMA((2, 4)),
+            pltpu.SemaphoreType.DMA((2,)),
+        ],
+        compiler_params=pltpu.CompilerParams(collective_id=0, has_side_effects=True, vmem_limit_bytes=48 << 20),
+    )(data, taps, scale)
+
+
+def scatter_kernel(seqs, dps, data_ref, grad_ref, got_ref, grad_got_ref, scale_got_ref,
+                   held, rows, sems, local_sems):
+    seq, dp = lax.axis_index("seq"), lax.axis_index("dp")
+    mine = seq * dps + dp
+    pairs = dps // 2
+    pair, parity = dp // 2, lax.rem(dp, 2)
+    greet(seqs, dps, seq, dp)
+
+    def send_grad(offset, carry):
+        peer_seq = lax.rem(seq + offset // 2, seqs)
+        peer_dp = pair * 2 + lax.rem(parity + offset, 2)
+        to_peer(grad_ref.at[peer_seq], held.at[parity * seqs + seq], sems, 0, peer_seq, peer_dp).start()
+        return carry
+
+    lax.fori_loop(1, 2 * seqs, send_grad, 0)
+    send_all(seqs, dps, seq, dp, data_ref, got_ref, sems, 1)
+    own = pltpu.make_async_copy(data_ref.at[mine], got_ref.at[mine], local_sems.at[0])
+    own.start()
+    own_grad = pltpu.make_async_copy(grad_ref.at[seq], held.at[parity * seqs + seq], local_sems.at[1])
+    own_grad.start()
+
+    next_seq = lax.rem(seq + 1, seqs)
+    rest = pl.ds(0, 2 * seqs - 1)
+    to_peer(held.at[rest], held.at[rest], sems, 0, next_seq, dp).wait()
+    own.wait()
+    own_grad.wait()
+    for other in range(pairs):
+        rows[other] = held[:, SUB + other * 2 + parity]
+
+    def send_along(offset, carry):
+        peer = lax.rem(pair + offset, pairs)
+        peer_dp = peer * 2 + parity
+        to_peer(held.at[:, pl.ds(0, SUB)], grad_got_ref.at[pair], sems, 2, seq, peer_dp).start()
+        to_peer(rows.at[peer], scale_got_ref.at[pair], sems, 3, seq, peer_dp).start()
+        return carry
+
+    lax.fori_loop(1, pairs, send_along, 0)
+    own_held = pltpu.make_async_copy(held.at[:, pl.ds(0, SUB)], grad_got_ref.at[pair], local_sems.at[0])
+    own_held.start()
+    own_rows = pltpu.make_async_copy(rows.at[pair], scale_got_ref.at[pair], local_sems.at[1])
+    own_rows.start()
+    rest_pairs = pl.ds(0, pairs - 1)
+    next_dp = lax.rem(dp + 2, dps)
+    to_peer(grad_got_ref.at[rest_pairs], grad_got_ref.at[rest_pairs], sems, 2, seq, next_dp).wait()
+    to_peer(scale_got_ref.at[rest_pairs], scale_got_ref.at[rest_pairs], sems, 3, seq, next_dp).wait()
+    rest_all = pl.ds(0, seqs * dps - 1)
+    to_peer(got_ref.at[rest_all], got_ref.at[rest_all], sems, 1, next_seq, dp).wait()
+    own_held.wait()
+    own_rows.wait()
+
+
+def scatter(data, grad, dps):
+    seqs = grad.shape[0]
+    pairs = dps // 2
+    vmem = pl.BlockSpec(memory_space=pltpu.VMEM)
+    return pl.pallas_call(
+        functools.partial(scatter_kernel, seqs, dps),
+        out_shape=(
+            jax.ShapeDtypeStruct(data.shape, data.dtype),
+            jax.ShapeDtypeStruct((pairs, 2 * seqs, SUB, LANES), jnp.float32),
+            jax.ShapeDtypeStruct((pairs, 2 * seqs, LANES), jnp.float32),
+        ),
+        in_specs=[vmem] * 2,
+        out_specs=(vmem,) * 3,
+        scratch_shapes=[
+            pltpu.VMEM((2 * seqs, 2 * SUB, LANES), jnp.float32),
+            pltpu.VMEM((pairs, 2 * seqs, LANES), jnp.float32),
+            pltpu.SemaphoreType.DMA((2, 4)),
+            pltpu.SemaphoreType.DMA((2,)),
+        ],
+        compiler_params=pltpu.CompilerParams(collective_id=1, has_side_effects=True, vmem_limit_bytes=48 << 20),
+    )(data, grad)
+
+
 def by_channel(value):
     return value.reshape(SUB, LANES, value.shape[-1]).transpose(2, 0, 1)
 
@@ -191,33 +366,25 @@
 def on_device(activations, gate_values, output_grad, filter_codes, filter_scales):
     channels = filter_codes.shape[1]
     seqs, replicas = lax.axis_size("seq"), lax.axis_size("dp")
-    replica = lax.axis_index("dp")
     block_size = filter_codes.shape[0] // filter_scales.shape[0]
     grad_in = output_grad[0].astype(jnp.float32)
     act = grad_in * gate_values[0].astype(jnp.float32)
     top = jnp.maximum(jnp.max(jnp.abs(act)), FLOOR)
-    scale_all = lax.all_gather((top * (1.0 / TOP8)).reshape(1), BOTH, tiled=True)
     act_code = eighth_power(act * (TOP8 / top)).astype(jnp.bfloat16)
     sent = jnp.concatenate([by_channel(activations[0]), by_channel(act_code)], axis=1)
-    got = lax.all_to_all(sent, BOTH, 0, 0, tiled=True)
-
     scale_rows = jnp.repeat(filter_scales, block_size, axis=0)
     taps = by_channel(filter_codes.astype(jnp.float32) * scale_rows)
-    taps_mine = lax.dynamic_index_in_dim(taps.reshape(seqs, replicas, SUB, LANES), replica, 1, keepdims=False)
-    taps_got = lax.all_to_all(taps_mine, "seq", 0, 0, tiled=True)
-
-    out, out_scale, grad = transforms(
-        scale_all, got.reshape(seqs, replicas, 2 * SUB, LANES), taps_got.reshape(ROWS, LANES)
+    got, taps_got, scales_got = gather(
+        sent, taps.reshape(seqs, replicas, SUB, LANES), jnp.full((SUB, LANES), top * (1.0 / TOP8), jnp.float32)
     )
-    out_scale_all = lax.all_gather(out_scale[:, :, 0], BOTH)
-    back = lax.all_to_all(out.reshape(channels, 2 * SUB, LANES), BOTH, 0, 0, tiled=True)
-    grad_seq = lax.all_to_all(grad.reshape(seqs, SUB, LANES), "seq", 0, 0, tiled=True)
-    grad_all = lax.all_gather(grad_seq, "dp", axis=1).reshape(channels, SUB, LANES)
-
-    my_scale = lax.dynamic_index_in_dim(out_scale_all, replica, 1, keepdims=False)
+    out, grad = transforms(scales_got, got.reshape(seqs, replicas, 2 * SUB, LANES), taps_got.reshape(ROWS, LANES))
+    back, grad_all, scale_all = scatter(out.reshape(channels, 2 * SUB, LANES), grad, replicas)
+    grad_all = grad_all.reshape(replicas // 2, 2, seqs, SUB, LANES).transpose(2, 0, 1, 3, 4).reshape(channels, SUB, LANES)
+    scale_all = scale_all.reshape(replicas // 2, 2, seqs, LANES).transpose(2, 0, 1, 3).reshape(channels, LANES)
+
     back = back.astype(jnp.float32)
-    conv = by_position(root_of(back[:, :SUB], 4) * my_scale[:, 0, None, None])
-    input_grad = by_position(root_of(back[:, SUB:], 3) * my_scale[:, 1, None, None])
+    conv = by_position(root_of(back[:, :SUB], 4) * scale_all[:, 0, None, None])
+    input_grad = by_position(root_of(back[:, SUB:], 3) * scale_all[:, LANES // 2, None, None])
     gate_grad = (grad_in * conv).astype(jnp.bfloat16)
     code_grad = by_position(grad_all) * scale_rows
     return (input_grad[None], gate_grad[None], code_grad)

time: 860 us -> 129 us (0.15)
  blocking collectives: 784 us -> 0 us
  Pallas kernels: 14.2 us -> 111 us
  starting transfers between devices: 26.8 us -> 0 us
  between operations: 15 us -> 1.55 us
    all_gather x1 -> x0, blocking collectives: 689 us -> none  [on_device(): out_scale_all = lax.all_gather(out_scale[:, :, 0], BOTH)]
    pallas_call x0 -> x2, Pallas kernels: none -> 97.9 us  [the longest x1 49.2 us: gather(): pl.pallas_call(functools.partial(gather_kernel, seqs, dps), out_shape=(ja...]
    unnamed x1 -> x0, blocking collectives: 79.9 us -> none
    all_to_all x3 -> x0, starting transfers between devices: 26.7 us -> none  [the longest x1 10.2 us: on_device(): got = lax.all_to_all(sent, BOTH, 0, 0, tiled=True)]
    all_to_all x1 -> x0, blocking collectives: 14.3 us -> none  [on_device(): lax.all_to_all(grad.reshape(seqs, SUB, LANES), 'seq', 0, 0, tiled=True)]
  transfers between devices with their start and end apart: 4 -> 0, of which waited for: 1 -> 0; matrix products, arithmetic and copies ran while one was open for 1% -> 0% of each run, Pallas kernels for 0% -> 0%
where the time goes in v2:
time: 129 us
  Pallas kernels  111 us (86%)
  local copies, waits for them, and re-layouts  9.12 us (7%)
  other arithmetic  7.77 us (6%)
  between operations  1.55 us (1%)
    pallas_call x1, Pallas kernels, gather(): pl.pallas_call(functools.partial(gather_kernel, seqs, dps), out_shape=(ja...  49.2 us
    pallas_call x1, Pallas kernels, scatter(): pl.pallas_call(functools.partial(scatter_kernel, seqs, dps), out_shape=(j...  48.7 us
    pallas_call x1, Pallas kernels, transforms(): pl.pallas_call(transform_kernel, out_shape=(jax.ShapeDtypeStruct(data.sha...  12.6 us
    unnamed x21, local copies, waits for them, and re-layouts  3.16 us

profile of v2, /device:TPU:1, one launch (start us, length us, event | category | flops | bytes accessed | tf_op | source)
XLA Modules:
  0.0 129.0 jit_solution(5045913440257776507)
XLA Ops:
  0.6 0.0 copy-start.5
  0.6 0.0 copy-start.7
  0.7 2.0 %abs_reduce_fusion = f32[]{:T(128)} fusion(bf16[1,1024,256]{2,1,0:T(8,128)(2,1)} %param.11, bf16[1,1024,256]{2,1,0:T(8,128)(2,1)} %param.12), kind=kLoop, calls=%fused_computation.16 | loop fusion | flops 1310719 | bytes 1048580 | tf_op jit(solution)/shard_map/reduce_max | solution.py:372
  3.4 1.4 %copy.26 = bf16[8,128,256]{1,0,2:T(8,128)(2,1)S(1)} copy(bf16[8,128,256]{2,1,0:T(8,128)(2,1)} %bitcast.48) | data formatting | bytes 1048576 | tf_op jit(solution)/shard_map/reshape;squeeze | solution.py:359
  4.7 0.0 copy-done.5
  4.7 0.0 copy-done.7
  4.8 0.1 fusion.8
  4.9 0.4 copy.27
  5.3 0.0 copy-start.8
  5.3 0.0 copy-start.9
  5.3 0.2 fusion.9
  5.6 0.2 pad_maximum_fusion.data_ref
  5.8 0.6 copy-done.8
  6.4 0.0 copy-done.9
  6.4 1.0 bitcast_multiply_fusion.1
  7.4 0.0 copy-start
  7.4 0.0 copy-start.1
  7.4 0.0 copy-start.2
  7.4 1.8 %copy.20 = f32[8,128,256]{1,0,2:T(8,128)S(1)} copy(f32[8,128,256]{2,1,0:T(8,128)} %bitcast.44) | data formatting | bytes 2097152 | tf_op jit(solution)/shard_map/reshape | solution.py:359
  9.2 0.0 copy-start.3
  9.2 0.0 copy-start.4
  9.2 49.2 %shard_map.121 = (bf16[256,16,128]{2,1,0:T(8,128)(2,1)S(1)}, f32[32,8,128]{2,1,0:T(8,128)S(1)}, f32[32,8,128]{2,1,0:T(8,128)S(1)}) custom-call(bf16[256,16,128]{2,1,0:T(8,128)(2,1)S(1)} %pad_maximum_fusion.data_ref, f32[32,8,8,128]{3,2,1,0:T(8,128)S(1)} %bitcast.35, f32[8,128]{1,0:T(8,128)S(1)} %broadcast_in_dim.8.scale_ref), custom_call_target="tpu_custom_call" | custom-call | tf_op jit(solution)/shard_map/pallas_call | solution.py:265
  58.4 0.0 copy-done
  58.5 0.0 copy-done.1
  58.5 0.0 copy-done.2
  58.5 0.0 copy-done.3
  58.5 0.0 copy-done.4
  58.5 12.6 %shard_map.122 = (bf16[32,8,16,128]{3,2,1,0:T(8,128)(2,1)S(1)}, f32[32,16,128]{2,1,0:T(8,128)S(1)}) custom-call(f32[32,8,128]{2,1,0:T(8,128)S(1)} %get-tuple-element.11.scale_ref, bf16[32,8,16,128]{3,2,1,0:T(8,128)(2,1)S(1)} %bitcast.39, f32[256,128]{1,0:T(8,128)S(1)} %bitcast.40, bf16[1024,256]{1,0:T(8,128)(2,1)S(1)} %copy-done.1, ...), custom_call_target="tpu_custom_call" | custom-call | flops 7000000000 | bytes 5000000 | tf_op jit(solution)/shard_map/pallas_call | solution.py:169
  71.1 48.7 %shard_map.123 = (bf16[256,16,128]{2,1,0:T(8,128)(2,1)S(1)}, f32[4,64,8,128]{3,2,1,0:T(8,128)S(1)}, f32[4,64,128]{2,1,0:T(8,128)S(1)}) custom-call(bf16[256,16,128]{2,1,0:T(8,128)(2,1)S(1)} %bitcast.36, f32[32,16,128]{2,1,0:T(8,128)S(1)} %get-tuple-element.15.grad_ref), custom_call_target="tpu_custom_call" | custom-call | tf_op jit(solution)/shard_map/pallas_call | solution.py:339
  119.8 0.1 copy.21
  119.9 0.2 slice_reduce_fusion
  120.1 0.2 convert_element_type.31
  120.3 2.0 %fusion.7 = (f32[8,128,256]{1,0,2:T(8,128)}, f32[8,128,256]{1,0,2:T(8,128)}) fusion(f32[256,16,128]{2,1,0:T(8,128)S(1)} %convert_element_type.31, f32[256]{0:T(256)S(1)} %get-tuple-element.25, f32[256]{0:T(256)S(1)} %get-tuple-element.26), kind=kLoop, calls=%fused_computation.14 | loop fusion | flops 3145728 | bytes 4196352 | tf_op jit(solution)/shard_map/transpose | solution.py:363
  122.3 0.0 copy-start.6
  122.3 1.6 %copy.29 = f32[8,128,256]{2,1,0:T(8,128)S(1)} copy(f32[8,128,256]{1,0,2:T(8,128)} %get-tuple-element.27) | data formatting | bytes 2097152 | tf_op jit(solution)/shard_map/reshape | solution.py:363
  123.9 0.0 copy-done.6
  123.9 0.9 fusion
  124.8 2.5 %copy.28 = f32[8,128,256]{2,1,0:T(8,128)} copy(f32[8,128,256]{1,0,2:T(8,128)} %get-tuple-element.28) | data formatting | bytes 2097152
  127.4 0.1 copy.23
  127.5 0.4 copy.30
  127.9 1.1 bitcast_multiply_fusion
  (1 shorter events, 0.0 us)
Async XLA Ops:
  0.6 4.1 %copy-start.5 = (bf16[1,1024,256]{2,1,0:T(8,128)(2,1)S(1)}, bf16[1,1024,256]{2,1,0:T(8,128)(2,1)}, u32[]{:S(2)}) copy-start(bf16[1,1024,256]{2,1,0:T(8,128)(2,1)} %param.12) | copy-start | bytes 1572868
  0.6 4.1 %copy-start.7 = (bf16[1,1024,256]{2,1,0:T(8,128)(2,1)S(1)}, bf16[1,1024,256]{2,1,0:T(8,128)(2,1)}, u32[]{:S(2)}) copy-start(bf16[1,1024,256]{2,1,0:T(8,128)(2,1)} %param.11) | copy-start | bytes 1572868
  5.3 1.0 copy-start.8
  5.3 1.0 copy-start.9
  7.4 51.0 %copy-start = (bf16[512,512]{1,0:T(8,128)(2,1)S(1)}, bf16[512,512]{1,0:T(8,128)(2,1)}, u32[]{:S(2)}) copy-start(bf16[512,512]{1,0:T(8,128)(2,1)} %constant.31.clone.last_ref) | copy-start | bytes 1572868
  7.4 51.0 %copy-start.1 = (bf16[1024,256]{1,0:T(8,128)(2,1)S(1)}, bf16[1024,256]{1,0:T(8,128)(2,1)}, u32[]{:S(2)}) copy-start(bf16[1024,256]{1,0:T(8,128)(2,1)} %constant.30.clone.first_ref) | copy-start | bytes 1572868
  7.4 51.0 %copy-start.2 = (f32[2,256,128]{2,1,0:T(8,128)S(1)}, f32[2,256,128]{2,1,0:T(8,128)}, u32[]{:S(2)}) copy-start(f32[2,256,128]{2,1,0:T(8,128)} %constant.34.clone.twist_ref) | copy-start | bytes 786436
  9.2 49.3 %copy-start.3 = (bf16[2,256,256]{2,1,0:T(8,128)(2,1)S(1)}, bf16[2,256,256]{2,1,0:T(8,128)(2,1)}, u32[]{:S(2)}) copy-start(bf16[2,256,256]{2,1,0:T(8,128)(2,1)} %constant.33.clone.backward_ref) | copy-start | bytes 786436
  9.2 49.3 %copy-start.4 = (bf16[2,256,256]{2,1,0:T(8,128)(2,1)S(1)}, bf16[2,256,256]{2,1,0:T(8,128)(2,1)}, u32[]{:S(2)}) copy-start(bf16[2,256,256]{2,1,0:T(8,128)(2,1)} %constant.32.clone.forward_ref) | copy-start | bytes 786436
  122.3 1.6 %copy-start.6 = (bf16[1,1024,256]{2,1,0:T(8,128)(2,1)S(1)}, bf16[1,1024,256]{2,1,0:T(8,128)(2,1)}, u32[]{:S(2)}) copy-start(bf16[1,1024,256]{2,1,0:T(8,128)(2,1)} %param.12) | copy-start | bytes 1572868

commit v3 on v1

v3 whole, which is shorter than its diff:
```python
import functools

import jax
import jax.numpy as jnp
import numpy as np
from jax import lax
from jax.experimental import pallas as pl
from jax.experimental.pallas import tpu as pltpu
from jax.sharding import PartitionSpec as P

LANES = 128
SUB = 8
ROWS = 256
FLOOR = 2.0**-90
TOP8 = 2.0**15
TOP12 = 2.0**2.5
TOP8_RMS = 2.0**7.75
RMS_FLOOR = 2.0**-50


def split_np(table):
    high = np.asarray(table, np.float64).astype(jnp.bfloat16)
    low = (np.asarray(table, np.float64) - high.astype(np.float64)).astype(jnp.bfloat16)
    return high, low


def tables():
    whole = 2 * ROWS * LANES
    rows = np.arange(ROWS, dtype=np.float64)
    lanes = np.arange(LANES, dtype=np.float64)
    outer = 2 * np.pi * (rows[:, None] + 0.5) * rows[None, :] / (2 * ROWS)
    first = np.concatenate([np.cos(outer), -np.sin(outer)], axis=0)
    last = np.concatenate([np.cos(outer.T), -np.sin(outer.T)], axis=1) * (2.0 / whole)
    inner = 2 * np.pi * lanes[:, None] * lanes[None, :] / LANES
    cos, sin = np.cos(inner), np.sin(inner)
    forward = np.block([[cos, -sin], [sin, cos]])
    backward = np.block([[cos, sin], [-sin, cos]])
    turn = 2 * np.pi * (rows[:, None] + 0.5) * lanes[None, :] / whole
    twist = np.stack([np.cos(turn), -np.sin(turn)]).astype(np.float32)
    first_hi, first_lo = split_np(first)
    last_hi, last_lo = split_np(last)
    return (
        np.concatenate([first_hi, first_lo], axis=0),
        np.concatenate([last_hi, last_lo], axis=0),
        np.stack(split_np(forward)),
        np.stack(split_np(backward)),
        twist,
    )


def dot(left, right):
    return jnp.dot(left, right, preferred_element_type=jnp.float32)


def halves(value):
    high = value.astype(jnp.bfloat16)
    low = (value - high.astype(jnp.float32)).astype(jnp.bfloat16)
    return high, low


def left_product(table_ref, high, low):
    count = table_ref.shape[0] // 2
    both = dot(table_ref[...], high)
    total = both[:count] + both[count:]
    if low is not None:
        total = total + dot(table_ref[:count], low)
    return total


def right_product(value, table_ref):
    high, low = halves(value)
    return dot(high, table_ref[0]) + dot(low, table_ref[0]) + dot(high, table_ref[1])


def forward(high, low, first_ref, forward_ref, twist_ref):
    section = left_product(first_ref, high, low)
    cos, sin = twist_ref[0], twist_ref[1]
    out = []
    for start in range(0, high.shape[1], LANES):
        real = section[:ROWS, start : start + LANES]
        imag = section[ROWS:, start : start + LANES]
        turned = jnp.concatenate([real * cos - imag * sin, real * sin + imag * cos], axis=1)
        out.append(right_product(turned, forward_ref))
    return out


def inverse(spectra, last_ref, backward_ref, twist_ref):
    cos, sin = twist_ref[0], twist_ref[1]
    sections = []
    for spec in spectra:
        part = right_product(spec, backward_ref)
        real, imag = part[:, :LANES], part[:, LANES:]
        sections.append(jnp.concatenate([real * cos + imag * sin, imag * cos - real * sin], axis=0))
    high, low = halves(jnp.concatenate(sections, axis=1))
    result = left_product(last_ref, high, low)
    return [result[:, i * LANES : (i + 1) * LANES] for i in range(len(spectra))]


def times(left, right):
    lr, li, rr, ri = left[:, :LANES], left[:, LANES:], right[:, :LANES], right[:, LANES:]
    return jnp.concatenate([lr * rr - li * ri, lr * ri + li * rr], axis=1)


def times_conj(left, right):
    lr, li, rr, ri = left[:, :LANES], left[:, LANES:], right[:, :LANES], right[:, LANES:]
    return jnp.concatenate([lr * rr + li * ri, li * rr - lr * ri], axis=1)


def eighth_power(value):
    two = value * value
    four = two * two
    return four * two * value * jnp.abs(value)


def twelfth_power(value):
    two = value * value
    four = two * two
    return four * four * two * value * jnp.abs(value)


def root_of(code, power):
    size = jnp.exp2(jnp.log2(jnp.abs(code)) * (1.0 / power))
    return jnp.where(code < 0, -size, size)


def root_mean_square(spec):
    whole = 2 * ROWS * LANES
    return jnp.sqrt(jnp.sum(spec * spec, keepdims=True) * (2.0 / whole)) * (1.0 / whole) ** 0.5


def to_peer(source, target, send_sem, recv_sem, seq, dp):
    return pltpu.make_async_remote_copy(
        src_ref=source, dst_ref=target, send_sem=send_sem, recv_sem=recv_sem,
        device_id={"seq": seq, "dp": dp}, device_id_type=pl.DeviceIdType.MESH,
    )


def greet(seqs, dps, seq, dp, ready):
    barrier = pltpu.get_barrier_semaphore()
    chips = seqs // 2
    core, chip = lax.rem(seq, 2), seq // 2
    near = 2 * dps

    def tell(sem, seq_to, dp_to):
        pl.semaphore_signal(sem, inc=1, device_id={"seq": seq_to, "dp": dp_to}, device_id_type=pl.DeviceIdType.MESH)

    def tell_near(offset, carry):
        peer = lax.rem(core * dps + dp + offset, near)
        tell(barrier, chip * 2 + peer // dps, lax.rem(peer, dps))
        return carry

    def tell_far(sem):
        def body(offset, carry):
            tell(sem, lax.rem(chip + offset, chips) * 2 + core, dp)
            return carry

        return body

    lax.fori_loop(1, chips, tell_far(barrier), 0)
    lax.fori_loop(1, near, tell_near, 0)
    pl.semaphore_wait(barrier, near + chips - 2)
    lax.fori_loop(1, chips, tell_far(ready), 0)
    pl.semaphore_wait(ready, chips - 1)


SCALE, TAPS, SCALES, GRAD, RMS, BACK, GRAD_Y, RMS_Y, DATA = range(9)


def main_kernel(
    seqs, dps, data_ref, taps_ref, scale_ref, first_ref, last_ref, forward_ref, backward_ref, twist_ref,
    back_ref, grad_all_ref, rms_all_ref,
    got, taps_got, scale_got, scale_row, scales_got, conv_specs, back_specs, cross_ref, out, grad, rms, held, held_rms,
    send_sems, recv_sems, local_sems, ready,
):
    seq, dp = lax.axis_index("seq"), lax.axis_index("dp")
    mine = seq * dps + dp
    pairs = dps // 2
    pair, parity = dp // 2, lax.rem(dp, 2)
    next_seq = lax.rem(seq + 1, seqs)
    lane = lax.broadcasted_iota(jnp.int32, (1, LANES), 1)
    group = LANES // dps
    half_group = group // 2

    def copy_to(source, target, kind, seq_to, dp_to, recv_kind=None):
        return to_peer(
            source, target, send_sems.at[kind], recv_sems.at[kind if recv_kind is None else recv_kind], seq_to, dp_to
        )

    def of(ref, count, kind, recv_kind=None):
        part = ref.at[pl.ds(0, count)]
        return copy_to(part, part, kind, next_seq, dp, recv_kind)

    greet(seqs, dps, seq, dp, ready)

    def send_scale(offset, carry):
        copy_to(scale_ref, scale_got.at[dp], SCALE, seq, lax.rem(dp + offset, dps)).start()
        return carry

    lax.fori_loop(1, dps, send_scale, 0)

    def send_taps(offset, carry):
        peer = lax.rem(seq + offset, seqs)
        copy_to(taps_ref.at[peer, dp], taps_got.at[seq], TAPS, peer, dp).start()
        return carry

    lax.fori_loop(1, seqs, send_taps, 0)

    def send_pair(step, source_of, target, kind, recv_kind):
        peer_pair = lax.rem(pair + step, pairs)

        def send(offset, carry):
            peer_seq = lax.rem(seq + offset // 2, seqs)
            peer_dp = peer_pair * 2 + lax.rem(parity + offset, 2)
            copy_to(source_of(peer_seq, peer_dp), target.at[mine], kind, peer_seq, peer_dp, recv_kind).start()
            return carry

        lax.fori_loop(jnp.where(step == 0, 1, 0), 2 * seqs, send, 0)

    def send_data(step, carry):
        send_pair(step, lambda s, d: data_ref.at[s * dps + d], got, DATA, DATA + pair)
        return carry

    lax.fori_loop(0, pairs, send_data, 0)
    own = pltpu.make_async_copy(data_ref.at[mine], got.at[mine], local_sems.at[0])
    own.start()
    own_taps = pltpu.make_async_copy(taps_ref.at[seq, dp], taps_got.at[seq], local_sems.at[1])
    own_taps.start()

    of(scale_got, dps - 1, SCALE).wait()
    scale_got[dp] = scale_ref[...]
    row = jnp.zeros((1, LANES), jnp.float32)
    for other in range(dps):
        row = jnp.where(lane // group == other, scale_got[other], row)
    scale_row[...] = row

    def send_row(offset, carry):
        copy_to(scale_row, scales_got.at[seq], SCALES, lax.rem(seq + offset, seqs), dp).start()
        return carry

    lax.fori_loop(1, seqs, send_row, 0)

    own_taps.wait()
    of(taps_got, seqs - 1, TAPS).wait()
    taps_high, taps_low = halves(taps_got[...].reshape(ROWS, LANES))
    (taps_spec,) = forward(taps_high, taps_low, first_ref, forward_ref, twist_ref)
    cross_ref[...] = jnp.zeros_like(cross_ref)
    own.wait()
    of(scales_got, seqs - 1, SCALES).wait()
    scales_got[seq] = scale_row[...]
    of(got, 2 * seqs - 1, DATA, DATA + pair).wait_recv()
    rms[...] = jnp.zeros_like(rms)

    def transform_pair(step, carry):
        source = lax.rem(pair + pairs - step, pairs)

        @pl.when(step > 0)
        def _():
            of(got, 2 * seqs, DATA, DATA + source).wait_recv()

        signals, acts = [], []
        for half in range(2):
            index = source * 2 + half
            tile = jnp.stack([got[s * dps + index] for s in range(seqs)]).astype(jnp.float32)
            signals.append(tile[:, :SUB].reshape(ROWS, LANES).astype(jnp.bfloat16))
            scale = jnp.max(jnp.where(lane // group == index, scales_got[...], 0.0), axis=-1, keepdims=True)
            acts.append((root_of(tile[:, SUB:], 8) * scale).reshape(ROWS, LANES))
        act_high, act_low = halves(jnp.concatenate(acts, axis=1))
        signal_specs = forward(jnp.concatenate(signals, axis=1), None, first_ref, forward_ref, twist_ref)
        act_specs = forward(act_high, act_low, first_ref, forward_ref, twist_ref)
        for half, (signal_spec, act_spec) in enumerate(zip(signal_specs, act_specs)):
            index = source * 2 + half
            cross_ref[...] += times_conj(act_spec, signal_spec)
            conv_spec, back_spec = times(signal_spec, carry), times_conj(act_spec, carry)
            conv_specs[index] = conv_spec
            back_specs[index] = back_spec
            conv_rms = jnp.maximum(root_mean_square(conv_spec), RMS_FLOOR)
            back_rms = jnp.maximum(root_mean_square(back_spec), RMS_FLOOR)
            both = jnp.where(lane % group < half_group, conv_rms, back_rms)
            rms[...] = jnp.where(lane // group == index, both, rms[...])
        return carry

    taps_spec = lax.fori_loop(0, pairs, transform_pair, taps_spec)

    (grad_value,) = inverse([cross_ref[...]], last_ref, backward_ref, twist_ref)
    grad[...] = grad_value.reshape(seqs, SUB, LANES)

    def send_grad(offset, carry):
        peer_seq = lax.rem(seq + offset // 2, seqs)
        peer_dp = pair * 2 + lax.rem(parity + offset, 2)
        copy_to(grad.at[peer_seq], held.at[parity * seqs + seq], GRAD, peer_seq, peer_dp).start()
        copy_to(rms, held_rms.at[parity * seqs + seq], RMS, peer_seq, peer_dp).start()
        return carry

    lax.fori_loop(1, 2 * seqs, send_grad, 0)

    def invert_pair(step, carry):
        target = lax.rem(pair + step, pairs)
        convs = inverse([conv_specs[target * 2], conv_specs[target * 2 + 1]], last_ref, backward_ref, twist_ref)
        backs = inverse([back_specs[target * 2], back_specs[target * 2 + 1]], last_ref, backward_ref, twist_ref)
        for half in range(2):
            index = target * 2 + half
            here = (lane // group == index) & (lane % half_group == 0)
            both = jnp.where(here, rms[...], 0.0)
            conv_rms = jnp.sum(jnp.where(lane % group < half_group, both, 0.0), keepdims=True)
            back_rms = jnp.sum(jnp.where(lane % group < half_group, 0.0, both), keepdims=True)
            conv_code = twelfth_power(convs[half] * (TOP12 / conv_rms)).reshape(seqs, SUB, LANES)
            back_code = eighth_power(backs[half] * (TOP8_RMS / back_rms)).reshape(seqs, SUB, LANES)
            out[index] = jnp.concatenate([conv_code, back_code], axis=1).astype(jnp.bfloat16)
        send_pair(step, lambda s, d: out.at[d, s], back_ref, BACK, BACK)
        return carry

    lax.fori_loop(0, pairs, invert_pair, 0)
    own_back = pltpu.make_async_copy(out.at[dp, seq], back_ref.at[mine], local_sems.at[0])
    own_back.start()

    of(held, 2 * seqs - 1, GRAD).wait()
    of(held_rms, 2 * seqs - 1, RMS).wait()
    held[parity * seqs + seq] = grad[seq]
    held_rms[parity * seqs + seq] = rms[...]

    def send_along(offset, carry):
        peer_dp = lax.rem(pair + offset, pairs) * 2 + parity
        copy_to(held, grad_all_ref.at[pair], GRAD_Y, seq, peer_dp).start()
        copy_to(held_rms, rms_all_ref.at[pair], RMS_Y, seq, peer_dp).start()
        return carry

    lax.fori_loop(1, pairs, send_along, 0)
    own_held = pltpu.make_async_copy(held, grad_all_ref.at[pair], local_sems.at[1])
    own_held.start()
    own_rms = pltpu.make_async_copy(held_rms, rms_all_ref.at[pair], local_sems.at[2])
    own_rms.start()
    own_back.wait()
    own_held.wait()
    own_rms.wait()
    of(got, seqs * dps - 1, DATA).wait_send()
    of(grad_all_ref, pairs - 1, GRAD_Y).wait()
    of(rms_all_ref, pairs - 1, RMS_Y).wait()
    of(back_ref, seqs * dps - 1, BACK).wait()


def exchange(data, taps, scale):
    seqs, dps = taps.shape[0], taps.shape[1]
    pairs = dps // 2
    vmem = pl.BlockSpec(memory_space=pltpu.VMEM)
    f32, bf16 = jnp.float32, jnp.bfloat16
    return pl.pallas_call(
        functools.partial(main_kernel, seqs, dps),
        out_shape=(
            jax.ShapeDtypeStruct(data.shape, bf16),
            jax.ShapeDtypeStruct((pairs, 2 * seqs, SUB, LANES), f32),
            jax.ShapeDtypeStruct((pairs, 2 * seqs, 1, LANES), f32),
        ),
        in_specs=[vmem] * 8,
        out_specs=(vmem,) * 3,
        scratch_shapes=[
            pltpu.VMEM(data.shape, bf16),
            pltpu.VMEM((seqs, SUB, LANES), f32),
            pltpu.VMEM((dps, 1, LANES), f32),
            pltpu.VMEM((1, LANES), f32),
            pltpu.VMEM((seqs, 1, LANES), f32),
            pltpu.VMEM((dps, ROWS, 2 * LANES), f32),
            pltpu.VMEM((dps, ROWS, 2 * LANES), f32),
            pltpu.VMEM((ROWS, 2 * LANES), f32),
            pltpu.VMEM((dps, seqs, 2 * SUB, LANES), bf16),
            pltpu.VMEM((seqs, SUB, LANES), f32),
            pltpu.VMEM((1, LANES), f32),
            pltpu.VMEM((2 * seqs, SUB, LANES), f32),
            pltpu.VMEM((2 * seqs, 1, LANES), f32),
            pltpu.SemaphoreType.DMA((DATA + 1,)),
            pltpu.SemaphoreType.DMA((DATA + pairs,)),
            pltpu.SemaphoreType.DMA((3,)),
            pltpu.SemaphoreType.REGULAR,
        ],
        compiler_params=pltpu.CompilerParams(collective_id=0, has_side_effects=True, vmem_limit_bytes=48 << 20),
    )(data, taps, scale, *[jnp.asarray(t) for t in tables()])


def by_channel(value):
    return value.reshape(SUB, LANES, value.shape[-1]).transpose(2, 0, 1)


def by_position(value):
    return value.transpose(1, 2, 0).reshape(SUB * LANES, value.shape[0])


def on_device(activations, gate_values, output_grad, filter_codes, filter_scales):
    channels = filter_codes.shape[1]
    seqs, replicas = lax.axis_size("seq"), lax.axis_size("dp")
    block_size = filter_codes.shape[0] // filter_scales.shape[0]
    grad_in = output_grad[0].astype(jnp.float32)
    act = grad_in * gate_values[0].astype(jnp.float32)
    top = jnp.maximum(jnp.max(jnp.abs(act)), FLOOR)
    act_code = eighth_power(act * (TOP8 / top)).astype(jnp.bfloat16)
    sent = jnp.concatenate([by_channel(activations[0]), by_channel(act_code)], axis=1)
    scale_rows = jnp.repeat(filter_scales, block_size, axis=0)
    taps = by_channel(filter_codes.astype(jnp.float32) * scale_rows)
    back, grad_all, rms_all = exchange(
        sent, taps.reshape(seqs, replicas, SUB, LANES), jnp.full((1, LANES), top * (1.0 / TOP8), jnp.float32)
    )
    grad_all = grad_all.reshape(replicas // 2, 2, seqs, SUB, LANES).transpose(2, 0, 1, 3, 4).reshape(channels, SUB, LANES)
    rms_all = rms_all.reshape(replicas // 2, 2, seqs, LANES).transpose(2, 0, 1, 3).reshape(channels, replicas, 2, -1)
    rms_all = lax.dynamic_index_in_dim(rms_all[..., 0], lax.axis_index("dp"), 1, keepdims=False)

    back = back.astype(jnp.float32)
    conv = by_position(root_of(back[:, :SUB], 12) * (rms_all[:, 0] * (1.0 / TOP12))[:, None, None])
    input_grad = by_position(root_of(back[:, SUB:], 8) * (rms_all[:, 1] * (1.0 / TOP8_RMS))[:, None, None])
    gate_grad = (grad_in * conv).astype(jnp.bfloat16)
    code_grad = by_position(grad_all) * scale_rows
    return (input_grad[None], gate_grad[None], code_grad)


def solution(mesh):
    in_specs = (
        P("dp", "seq", None),
        P("dp", "seq", None),
        P("dp", "seq", None),
        P("seq", None),
        P("seq", None),
    )
    out_specs = (P("dp", "seq", None), P("dp", "seq", None), P("seq", None))
    return jax.shard_map(on_device, mesh=mesh, in_specs=in_specs, out_specs=out_specs, check_vma=False)
```

time: 860 us -> 113 us (0.13)
  blocking collectives: 784 us -> 0 us
  Pallas kernels: 14.2 us -> 88.5 us
  starting transfers between devices: 26.8 us -> 0 us
  between operations: 15 us -> 1.51 us
    all_gather x1 -> x0, blocking collectives: 689 us -> none  [on_device(): out_scale_all = lax.all_gather(out_scale[:, :, 0], BOTH)]
    unnamed x1 -> x0, blocking collectives: 79.9 us -> none
    pallas_call x1, Pallas kernels: 14.2 us -> 88.5 us  [exchange(): pl.pallas_call(functools.partial(main_kernel, seqs, dps), out_shape=(jax....]
    all_to_all x3 -> x0, starting transfers between devices: 26.7 us -> none  [the longest x1 10.2 us: on_device(): got = lax.all_to_all(sent, BOTH, 0, 0, tiled=True)]
    all_to_all x1 -> x0, blocking collectives: 14.3 us -> none  [on_device(): lax.all_to_all(grad.reshape(seqs, SUB, LANES), 'seq', 0, 0, tiled=True)]
  transfers between devices with their start and end apart: 4 -> 0, of which waited for: 1 -> 0; matrix products, arithmetic and copies ran while one was open for 1% -> 0% of each run, Pallas kernels for 0% -> 0%
where the time goes in v3:
time: 113 us; the launch traced here: 112 us
  Pallas kernels  88.5 us (78%)
  local copies, waits for them, and re-layouts  14.6 us (13%)
  other arithmetic  7.77 us (7%)
  between operations  1.51 us (1%)
    pallas_call x1, Pallas kernels, exchange(): pl.pallas_call(functools.partial(main_kernel, seqs, dps), out_shape=(jax....  88.5 us
    unnamed x23, local copies, waits for them, and re-layouts  8.91 us
    reshape x2, local copies, waits for them, and re-layouts, on_device(): rms_all.reshape(replicas // 2, 2, seqs, LANES).transpose(2, 0, 1, 3)  3.41 us

profile of v3, /device:TPU:1, one launch (start us, length us, event | category | flops | bytes accessed | tf_op | source)
XLA Modules:
  0.0 112.4 jit_solution(1632361220354765806)
XLA Ops:
  0.6 1.9 %abs_reduce_fusion = f32[]{:T(128)} fusion(bf16[1,1024,256]{2,1,0:T(8,128)(2,1)} %param.11, bf16[1,1024,256]{2,1,0:T(8,128)(2,1)} %param.12), kind=kLoop, calls=%fused_computation.16 | loop fusion | flops 1310719 | bytes 1048580 | tf_op jit(solution)/shard_map/reduce_max | solution.py:392
  3.3 1.3 %fusion.8 = f32[1,1024,256]{2,1,0:T(8,128)S(1)} fusion(bf16[1,1024,256]{2,1,0:T(8,128)(2,1)} %param.11, bf16[1,1024,256]{2,1,0:T(8,128)(2,1)} %param.12, f32[]{:T(128)S(6)} %div.3), kind=kLoop, calls=%fused_computation.17 | loop fusion | flops 1048576 | bytes 2097156 | tf_op jit(solution)/shard_map/mul | solution.py:393
  4.6 0.0 copy-start.9
  4.6 0.4 copy.28
  5.0 0.0 copy-start.8
  5.0 0.0 copy-start.10
  5.0 0.2 fusion.9
  5.3 0.3 copy-done.9
  5.6 0.3 copy.27
  6.0 0.2 pad_maximum_fusion.data_ref
  6.2 0.0 copy-start.4
  6.2 0.0 copy-done.8
  6.2 0.0 copy-done.10
  6.2 0.1 bitcast_multiply_fusion.1
  6.3 0.4 copy.20
  6.7 0.4 copy-done.4
  7.1 0.0 copy-start.2
  7.1 1.0 copy-done.2
  8.1 0.0 copy-start.3
  8.2 1.0 copy-done.3
  9.2 0.0 copy-start.5
  9.2 0.9 copy-done.5
  10.1 0.0 copy-start.6
  10.1 0.9 copy-done.6
  11.1 88.5 %shard_map.121 = (bf16[256,16,128]{2,1,0:T(8,128)(2,1)S(1)}, f32[4,64,8,128]{3,2,1,0:T(8,128)S(1)}, f32[4,64,1,128]{3,2,1,0:T(1,128)S(1)}) custom-call(bf16[256,16,128]{2,1,0:T(8,128)(2,1)S(1)} %pad_maximum_fusion.data_ref, f32[32,8,8,128]{3,2,1,0:T(8,128)S(1)} %bitcast.36, f32[1,128]{1,0:T(1,128)S(1)} %broadcast_in_dim.10.scale_ref, ...), custom_call_target="tpu_custom_call" | custom-call | tf_op jit(solution)/shard_map/pallas_call | solution.py:346
  99.6 0.0 copy-start
  99.6 1.0 copy-done
  100.6 0.1 copy.33
  100.7 3.3 %reshape.66 = f32[256,8,2,8]{3,2,1,0:T(2,128)S(1)} reshape(f32[32,4,2,128]{3,2,1,0:T(2,128)S(1)} %bitcast.46) | data formatting | bytes 262144 | tf_op jit(solution)/shard_map/reshape | solution.py:401
  104.0 0.1 constant_dynamic-slice_fusion
  104.1 0.1 copy.22
  104.3 0.2 convert_element_type.31
  104.4 1.9 %fusion.7 = (f32[8,128,256]{1,0,2:T(8,128)S(1)}, f32[8,128,256]{1,0,2:T(8,128)}) fusion(f32[256,16,128]{2,1,0:T(8,128)S(1)} %convert_element_type.31, f32[256]{0:T(256)S(1)} %bitcast.49, f32[256]{0:T(256)S(1)} %bitcast.50), kind=kLoop, calls=%fused_computation.14 | loop fusion | flops 3145728 | bytes 4196352 | tf_op jit(solution)/shard_map/transpose | solution.py:383
  106.3 0.0 copy-start.7
  106.3 0.4 copy.30
  106.7 0.6 copy-done.7
  107.4 0.0 copy-start.1
  107.4 0.9 fusion
  108.3 2.5 %copy.29 = f32[8,128,256]{2,1,0:T(8,128)} copy(f32[8,128,256]{1,0,2:T(8,128)} %get-tuple-element.16) | data formatting | bytes 2097152
  110.8 0.0 copy-done.1
  110.8 0.1 copy.24
  110.9 0.4 copy.31
  111.3 1.1 bitcast_multiply_fusion
  (2 shorter events, 0.0 us)
Async XLA Ops:
  4.6 1.0 copy-start.9
  5.0 1.2 %copy-start.8 = (bf16[1024,256]{1,0:T(8,128)(2,1)S(1)}, bf16[1024,256]{1,0:T(8,128)(2,1)}, u32[]{:S(2)}) copy-start(bf16[1024,256]{1,0:T(8,128)(2,1)} %param.13) | copy-start | bytes 1572868
  5.0 1.2 %copy-start.10 = (f32[8,256]{1,0:T(8,128)S(1)}, f32[8,256]{1,0:T(8,128)}, u32[]{:S(2)}) copy-start(f32[8,256]{1,0:T(8,128)} %param.14) | copy-start | bytes 24580
  6.2 1.0 copy-start.4
  7.1 1.0 copy-start.2
  8.1 1.0 copy-start.3
  9.2 0.9 copy-start.5
  10.1 0.9 copy-start.6
  99.6 1.0 copy-start
  106.3 1.0 copy-start.7
  107.4 3.4 %copy-start.1 = (f32[4,64,8,128]{3,2,1,0:T(8,128)S(1)}, f32[4,64,8,128]{3,2,1,0:T(8,128)}, u32[]{:S(2)}) copy-start(f32[4,64,8,128]{3,2,1,0:T(8,128)} %copy-done) | copy-start | bytes 3145732

commit v4 on v3

--- a/solution.py
+++ b/solution.py
@@ -13,7 +13,7 @@
 ROWS = 256
 FLOOR = 2.0**-90
 TOP8 = 2.0**15
-TOP12 = 2.0**2.5
+TOP14 = 2.0
 TOP8_RMS = 2.0**7.75
 RMS_FLOOR = 2.0**-50
 
@@ -112,10 +112,10 @@
     return four * two * value * jnp.abs(value)
 
 
-def twelfth_power(value):
+def fourteenth_power(value):
     two = value * value
     four = two * two
-    return four * four * two * value * jnp.abs(value)
+    return four * four * four * value * jnp.abs(value)
 
 
 def root_of(code, power):
@@ -135,7 +135,7 @@
     )
 
 
-def greet(seqs, dps, seq, dp, ready):
+def greet(seqs, dps, seq, dp, ready, meanwhile):
     barrier = pltpu.get_barrier_semaphore()
     chips = seqs // 2
     core, chip = lax.rem(seq, 2), seq // 2
@@ -158,28 +158,78 @@
 
     lax.fori_loop(1, chips, tell_far(barrier), 0)
     lax.fori_loop(1, near, tell_near, 0)
+    meanwhile()
     pl.semaphore_wait(barrier, near + chips - 2)
     lax.fori_loop(1, chips, tell_far(ready), 0)
     pl.semaphore_wait(ready, chips - 1)
 
 
 SCALE, TAPS, SCALES, GRAD, RMS, BACK, GRAD_Y, RMS_Y, DATA = range(9)
+CONV_LANE, GRAD_LANE, BACK_LANE = 0, 4, 8
+
+
+def lane_of(rows, lane, wanted):
+    return jnp.max(jnp.where(lane == wanted, rows, 0.0), axis=-1, keepdims=True)
 
 
 def main_kernel(
-    seqs, dps, data_ref, taps_ref, scale_ref, first_ref, last_ref, forward_ref, backward_ref, twist_ref,
+    seqs, dps, acts_hbm, gate_hbm, cot_hbm, codes_hbm, filter_scale_ref,
+    first_hbm, last_hbm, forward_hbm, backward_hbm, twist_hbm,
     back_ref, grad_all_ref, rms_all_ref,
+    acts_ref, gate_ref, cot_ref, codes_ref, first_ref, last_ref, forward_ref, backward_ref, twist_ref,
+    turned, taps_ref, data_ref, scale_ref,
     got, taps_got, scale_got, scale_row, scales_got, conv_specs, back_specs, cross_ref, out, grad, rms, held, held_rms,
-    send_sems, recv_sems, local_sems, ready,
+    grad_code, send_sems, recv_sems, local_sems, load_sems, ready,
 ):
     seq, dp = lax.axis_index("seq"), lax.axis_index("dp")
-    mine = seq * dps + dp
+    mine = dp * seqs + seq
     pairs = dps // 2
     pair, parity = dp // 2, lax.rem(dp, 2)
     next_seq = lax.rem(seq + 1, seqs)
     lane = lax.broadcasted_iota(jnp.int32, (1, LANES), 1)
     group = LANES // dps
-    half_group = group // 2
+    channels = seqs * dps
+
+    loads = [
+        pltpu.make_async_copy(source, target, load_sems.at[i])
+        for i, (source, target) in enumerate(
+            [(cot_hbm, cot_ref), (gate_hbm, gate_ref), (acts_hbm, acts_ref), (codes_hbm, codes_ref),
+             (twist_hbm, twist_ref), (first_hbm, first_ref), (forward_hbm, forward_ref),
+             (backward_hbm, backward_ref), (last_hbm, last_ref)]
+        )
+    ]
+    for load in loads:
+        load.start()
+
+    def turn():
+        for load in loads[:4]:
+            load.wait()
+
+        def chunk(i, top):
+            at = pl.ds(pl.multiple_of(i * LANES, LANES), LANES)
+            acts = acts_ref[at].astype(jnp.float32)
+            grads = cot_ref[at].astype(jnp.float32) * gate_ref[at].astype(jnp.float32)
+            taps = codes_ref[at].astype(jnp.float32) * filter_scale_ref[pl.ds(i, 1)]
+            for start in range(0, channels, LANES):
+                part = slice(start, start + LANES)
+                turned[pl.ds(start * 2 * SUB + i, LANES, stride=2 * SUB)] = acts[:, part].T
+                turned[pl.ds(start * 2 * SUB + SUB + i, LANES, stride=2 * SUB)] = grads[:, part].T
+                taps_ref[pl.ds(start * SUB + i, LANES, stride=SUB)] = taps[:, part].T
+            return jnp.maximum(top, jnp.max(jnp.abs(grads), axis=0, keepdims=True))
+
+        top = lax.fori_loop(0, SUB, chunk, jnp.zeros((1, channels), jnp.float32))
+        top = jnp.maximum(jnp.max(top, keepdims=True), FLOOR)
+        scale_ref[...] = jnp.broadcast_to(top * (1.0 / TOP8), (1, LANES))
+        factor = (TOP8 / top).reshape(1, 1, 1)
+
+        def code(i, carry):
+            tile = turned[pl.ds(pl.multiple_of(i * seqs * 2 * SUB, 2 * SUB), seqs * 2 * SUB)]
+            tile = tile.reshape(seqs, 2 * SUB, LANES)
+            coded = jnp.concatenate([tile[:, :SUB], eighth_power(tile[:, SUB:] * factor)], axis=1)
+            data_ref[pl.ds(i * seqs, seqs)] = coded.astype(jnp.bfloat16)
+            return carry
+
+        lax.fori_loop(0, dps, code, 0)
 
     def copy_to(source, target, kind, seq_to, dp_to, recv_kind=None):
         return to_peer(
@@ -190,7 +240,10 @@
         part = ref.at[pl.ds(0, count)]
         return copy_to(part, part, kind, next_seq, dp, recv_kind)
 
-    greet(seqs, dps, seq, dp, ready)
+    def taps_of(seq_to):
+        return taps_ref.at[pl.ds(pl.multiple_of((dp * seqs + seq_to) * SUB, SUB), SUB)]
+
+    greet(seqs, dps, seq, dp, ready, turn)
 
     def send_scale(offset, carry):
         copy_to(scale_ref, scale_got.at[dp], SCALE, seq, lax.rem(dp + offset, dps)).start()
@@ -200,7 +253,7 @@
 
     def send_taps(offset, carry):
         peer = lax.rem(seq + offset, seqs)
-        copy_to(taps_ref.at[peer, dp], taps_got.at[seq], TAPS, peer, dp).start()
+        copy_to(taps_of(peer), taps_got.at[seq], TAPS, peer, dp).start()
         return carry
 
     lax.fori_loop(1, seqs, send_taps, 0)
@@ -217,13 +270,13 @@
         lax.fori_loop(jnp.where(step == 0, 1, 0), 2 * seqs, send, 0)
 
     def send_data(step, carry):
-        send_pair(step, lambda s, d: data_ref.at[s * dps + d], got, DATA, DATA + pair)
+        send_pair(step, lambda s, d: data_ref.at[d * seqs + s], got, DATA, DATA + pair)
         return carry
 
     lax.fori_loop(0, pairs, send_data, 0)
     own = pltpu.make_async_copy(data_ref.at[mine], got.at[mine], local_sems.at[0])
     own.start()
-    own_taps = pltpu.make_async_copy(taps_ref.at[seq, dp], taps_got.at[seq], local_sems.at[1])
+    own_taps = pltpu.make_async_copy(taps_of(seq), taps_got.at[seq], local_sems.at[1])
     own_taps.start()
 
     of(scale_got, dps - 1, SCALE).wait()
@@ -239,6 +292,8 @@
 
     lax.fori_loop(1, seqs, send_row, 0)
 
+    for load in loads[4:]:
+        load.wait()
     own_taps.wait()
     of(taps_got, seqs - 1, TAPS).wait()
     taps_high, taps_low = halves(taps_got[...].reshape(ROWS, LANES))
@@ -260,9 +315,9 @@
         signals, acts = [], []
         for half in range(2):
             index = source * 2 + half
-            tile = jnp.stack([got[s * dps + index] for s in range(seqs)]).astype(jnp.float32)
+            tile = got[pl.ds(index * seqs, seqs)].astype(jnp.float32)
             signals.append(tile[:, :SUB].reshape(ROWS, LANES).astype(jnp.bfloat16))
-            scale = jnp.max(jnp.where(lane // group == index, scales_got[...], 0.0), axis=-1, keepdims=True)
+            scale = lane_of(scales_got[...], lane, index * group)
             acts.append((root_of(tile[:, SUB:], 8) * scale).reshape(ROWS, LANES))
         act_high, act_low = halves(jnp.concatenate(acts, axis=1))
         signal_specs = forward(jnp.concatenate(signals, axis=1), None, first_ref, forward_ref, twist_ref)
@@ -275,13 +330,17 @@
             back_specs[index] = back_spec
             conv_rms = jnp.maximum(root_mean_square(conv_spec), RMS_FLOOR)
             back_rms = jnp.maximum(root_mean_square(back_spec), RMS_FLOOR)
-            both = jnp.where(lane % group < half_group, conv_rms, back_rms)
+            both = jnp.where(lane % group < BACK_LANE, conv_rms, back_rms)
             rms[...] = jnp.where(lane // group == index, both, rms[...])
         return carry
 
-    taps_spec = lax.fori_loop(0, pairs, transform_pair, taps_spec)
-
-    (grad_value,) = inverse([cross_ref[...]], last_ref, backward_ref, twist_ref)
+    lax.fori_loop(0, pairs, transform_pair, taps_spec)
+
+    cross = cross_ref[...]
+    grad_rms = jnp.maximum(root_mean_square(cross), RMS_FLOOR)
+    in_group = lane % group
+    rms[...] = jnp.where((in_group >= GRAD_LANE) & (in_group < BACK_LANE), grad_rms, rms[...])
+    (grad_value,) = inverse([cross], last_ref, backward_ref, twist_ref)
     grad[...] = grad_value.reshape(seqs, SUB, LANES)
 
     def send_grad(offset, carry):
@@ -292,6 +351,22 @@
         return carry
 
     lax.fori_loop(1, 2 * seqs, send_grad, 0)
+
+    def send_along_y():
+        of(held, 2 * seqs - 1, GRAD).wait()
+        of(held_rms, 2 * seqs - 1, RMS).wait()
+        held[parity * seqs + seq] = grad[seq]
+        held_rms[parity * seqs + seq] = rms[...]
+        code = eighth_power(held[...] * (TOP8_RMS / lane_of(held_rms[...], lane, GRAD_LANE)))
+        grad_code[...] = code.reshape(seqs, 2 * SUB, LANES).astype(jnp.bfloat16)
+
+        def send_along(offset, carry):
+            peer_dp = lax.rem(pair + offset, pairs) * 2 + parity
+            copy_to(grad_code, grad_all_ref.at[pair], GRAD_Y, seq, peer_dp).start()
+            copy_to(held_rms, rms_all_ref.at[pair], RMS_Y, seq, peer_dp).start()
+            return carry
+
+        lax.fori_loop(1, pairs, send_along, 0)
 
     def invert_pair(step, carry):
         target = lax.rem(pair + step, pairs)
@@ -299,61 +374,58 @@
         backs = inverse([back_specs[target * 2], back_specs[target * 2 + 1]], last_ref, backward_ref, twist_ref)
         for half in range(2):
             index = target * 2 + half
-            here = (lane // group == index) & (lane % half_group == 0)
-            both = jnp.where(here, rms[...], 0.0)
-            conv_rms = jnp.sum(jnp.where(lane % group < half_group, both, 0.0), keepdims=True)
-            back_rms = jnp.sum(jnp.where(lane % group < half_group, 0.0, both), keepdims=True)
-            conv_code = twelfth_power(convs[half] * (TOP12 / conv_rms)).reshape(seqs, SUB, LANES)
+            conv_rms = lane_of(rms[...], lane, index * group + CONV_LANE)
+            back_rms = lane_of(rms[...], lane, index * group + BACK_LANE)
+            conv_code = fourteenth_power(convs[half] * (TOP14 / conv_rms)).reshape(seqs, SUB, LANES)
             back_code = eighth_power(backs[half] * (TOP8_RMS / back_rms)).reshape(seqs, SUB, LANES)
             out[index] = jnp.concatenate([conv_code, back_code], axis=1).astype(jnp.bfloat16)
+
+        @pl.when(step == 1)
+        def _():
+            send_along_y()
+
         send_pair(step, lambda s, d: out.at[d, s], back_ref, BACK, BACK)
         return carry
 
     lax.fori_loop(0, pairs, invert_pair, 0)
     own_back = pltpu.make_async_copy(out.at[dp, seq], back_ref.at[mine], local_sems.at[0])
     own_back.start()
-
-    of(held, 2 * seqs - 1, GRAD).wait()
-    of(held_rms, 2 * seqs - 1, RMS).wait()
-    held[parity * seqs + seq] = grad[seq]
-    held_rms[parity * seqs + seq] = rms[...]
-
-    def send_along(offset, carry):
-        peer_dp = lax.rem(pair + offset, pairs) * 2 + parity
-        copy_to(held, grad_all_ref.at[pair], GRAD_Y, seq, peer_dp).start()
-        copy_to(held_rms, rms_all_ref.at[pair], RMS_Y, seq, peer_dp).start()
-        return carry
-
-    lax.fori_loop(1, pairs, send_along, 0)
-    own_held = pltpu.make_async_copy(held, grad_all_ref.at[pair], local_sems.at[1])
-    own_held.start()
+    own_grad = pltpu.make_async_copy(grad_code, grad_all_ref.at[pair], local_sems.at[1])
+    own_grad.start()
     own_rms = pltpu.make_async_copy(held_rms, rms_all_ref.at[pair], local_sems.at[2])
     own_rms.start()
     own_back.wait()
-    own_held.wait()
+    own_grad.wait()
     own_rms.wait()
-    of(got, seqs * dps - 1, DATA).wait_send()
+    of(got, channels - 1, DATA).wait_send()
     of(grad_all_ref, pairs - 1, GRAD_Y).wait()
     of(rms_all_ref, pairs - 1, RMS_Y).wait()
-    of(back_ref, seqs * dps - 1, BACK).wait()
-
-
-def exchange(data, taps, scale):
-    seqs, dps = taps.shape[0], taps.shape[1]
-    pairs = dps // 2
-    vmem = pl.BlockSpec(memory_space=pltpu.VMEM)
+    of(back_ref, channels - 1, BACK).wait()
+
+
+def exchange(seqs, dps, acts, gate, cot, codes, filter_scales):
+    pairs, channels = dps // 2, seqs * dps
+    vmem, hbm = pl.BlockSpec(memory_space=pltpu.VMEM), pl.BlockSpec(memory_space=pl.ANY)
     f32, bf16 = jnp.float32, jnp.bfloat16
+    constants = [jnp.asarray(t) for t in tables()]
+    first, last, forward_table, backward_table, twist = constants
     return pl.pallas_call(
         functools.partial(main_kernel, seqs, dps),
         out_shape=(
-            jax.ShapeDtypeStruct(data.shape, bf16),
-            jax.ShapeDtypeStruct((pairs, 2 * seqs, SUB, LANES), f32),
+            jax.ShapeDtypeStruct((channels, 2 * SUB, LANES), bf16),
+            jax.ShapeDtypeStruct((pairs, seqs, 2 * SUB, LANES), bf16),
             jax.ShapeDtypeStruct((pairs, 2 * seqs, 1, LANES), f32),
         ),
-        in_specs=[vmem] * 8,
+        in_specs=[hbm] * 4 + [vmem] + [hbm] * 5,
         out_specs=(vmem,) * 3,
-        scratch_shapes=[
-            pltpu.VMEM(data.shape, bf16),
+        scratch_shapes=[pltpu.VMEM(value.shape, bf16) for value in (acts, gate, cot, codes)]
+        + [pltpu.VMEM(value.shape, value.dtype) for value in constants]
+        + [
+            pltpu.VMEM((channels * 2 * SUB, LANES), f32),
+            pltpu.VMEM((channels * SUB, LANES), f32),
+            pltpu.VMEM((channels, 2 * SUB, LANES), bf16),
+            pltpu.VMEM((1, LANES), f32),
+            pltpu.VMEM((channels, 2 * SUB, LANES), bf16),
             pltpu.VMEM((seqs, SUB, LANES), f32),
             pltpu.VMEM((dps, 1, LANES), f32),
             pltpu.VMEM((1, LANES), f32),
@@ -366,46 +438,83 @@
             pltpu.VMEM((1, LANES), f32),
             pltpu.VMEM((2 * seqs, SUB, LANES), f32),
             pltpu.VMEM((2 * seqs, 1, LANES), f32),
+            pltpu.VMEM((seqs, 2 * SUB, LANES), bf16),
             pltpu.SemaphoreType.DMA((DATA + 1,)),
             pltpu.SemaphoreType.DMA((DATA + pairs,)),
             pltpu.SemaphoreType.DMA((3,)),
+            pltpu.SemaphoreType.DMA((9,)),
             pltpu.SemaphoreType.REGULAR,
         ],
-        compiler_params=pltpu.CompilerParams(collective_id=0, has_side_effects=True, vmem_limit_bytes=48 << 20),
-    )(data, taps, scale, *[jnp.asarray(t) for t in tables()])
-
-
-def by_channel(value):
-    return value.reshape(SUB, LANES, value.shape[-1]).transpose(2, 0, 1)
-
-
-def by_position(value):
-    return value.transpose(1, 2, 0).reshape(SUB * LANES, value.shape[0])
+        compiler_params=pltpu.CompilerParams(collective_id=0, has_side_effects=True, vmem_limit_bytes=62 << 20),
+    )(acts, gate, cot, codes, filter_scales, first, last, forward_table, backward_table, twist)
+
+
+def finish_kernel(dps, back_ref, grad_ref, rms_ref, cot_ref, filter_scale_ref, input_ref, gate_ref, code_ref, turned, turned_grad):
+    step = pl.program_id(0)
+    channels = back_ref.shape[0]
+    block = channels // dps
+
+    @pl.when(step == 0)
+    def _():
+        lane = lax.broadcasted_iota(jnp.int32, (1, LANES), 1)
+        base = lax.axis_index("dp") * (LANES // dps)
+
+        def decode(i, carry):
+            at = pl.ds(i * block, block)
+            rms = rms_ref[at]
+            tile = back_ref[at].astype(jnp.float32)
+            conv = root_of(tile[:, :SUB], 14) * (lane_of(rms, lane, base + CONV_LANE) * (1.0 / TOP14))
+            back = root_of(tile[:, SUB:], 8) * (lane_of(rms, lane, base + BACK_LANE) * (1.0 / TOP8_RMS))
+            rows = pl.ds(pl.multiple_of(i * block * 2 * SUB, 2 * SUB), block * 2 * SUB)
+            turned[rows] = jnp.concatenate([conv, back], axis=1).reshape(block * 2 * SUB, LANES)
+            grad = grad_ref[pl.ds(i * (block // 2), block // 2)].astype(jnp.float32).reshape(block, SUB, LANES)
+            grad = root_of(grad, 8) * (lane_of(rms, lane, GRAD_LANE) * (1.0 / TOP8_RMS))
+            turned_grad[pl.ds(pl.multiple_of(i * block * SUB, SUB), block * SUB)] = grad.reshape(block * SUB, LANES)
+            return carry
+
+        lax.fori_loop(0, dps, decode, 0)
+
+    scales = filter_scale_ref[pl.ds(step, 1)]
+    for start in range(0, channels, LANES):
+        part = slice(start, start + LANES)
+        conv = turned[pl.ds(start * 2 * SUB + step, LANES, stride=2 * SUB)].T
+        gate_ref[:, part] = (cot_ref[:, part].astype(jnp.float32) * conv).astype(jnp.bfloat16)
+        input_ref[:, part] = turned[pl.ds(start * 2 * SUB + SUB + step, LANES, stride=2 * SUB)].T
+        grad = turned_grad[pl.ds(start * SUB + step, LANES, stride=SUB)].T
+        code_ref[:, part] = grad * scales[:, part]
+
+
+def finish(dps, back, grad, rms, cot, filter_scales):
+    channels = back.shape[0]
+    vmem = pl.BlockSpec(memory_space=pltpu.VMEM)
+    chunk = pl.BlockSpec((LANES, channels), lambda i: (i, 0))
+    return pl.pallas_call(
+        functools.partial(finish_kernel, dps),
+        grid=(SUB,),
+        out_shape=(
+            jax.ShapeDtypeStruct(cot.shape, jnp.float32),
+            jax.ShapeDtypeStruct(cot.shape, jnp.bfloat16),
+            jax.ShapeDtypeStruct(cot.shape, jnp.float32),
+        ),
+        in_specs=[vmem, vmem, vmem, chunk, vmem],
+        out_specs=(chunk,) * 3,
+        scratch_shapes=[
+            pltpu.VMEM((channels * 2 * SUB, LANES), jnp.float32),
+            pltpu.VMEM((channels * SUB, LANES), jnp.float32),
+        ],
+        compiler_params=pltpu.CompilerParams(vmem_limit_bytes=62 << 20),
+    )(back, grad, rms, cot, filter_scales)
 
 
 def on_device(activations, gate_values, output_grad, filter_codes, filter_scales):
+    seqs, dps = lax.axis_size("seq"), lax.axis_size("dp")
     channels = filter_codes.shape[1]
-    seqs, replicas = lax.axis_size("seq"), lax.axis_size("dp")
-    block_size = filter_codes.shape[0] // filter_scales.shape[0]
-    grad_in = output_grad[0].astype(jnp.float32)
-    act = grad_in * gate_values[0].astype(jnp.float32)
-    top = jnp.maximum(jnp.max(jnp.abs(act)), FLOOR)
-    act_code = eighth_power(act * (TOP8 / top)).astype(jnp.bfloat16)
-    sent = jnp.concatenate([by_channel(activations[0]), by_channel(act_code)], axis=1)
-    scale_rows = jnp.repeat(filter_scales, block_size, axis=0)
-    taps = by_channel(filter_codes.astype(jnp.float32) * scale_rows)
-    back, grad_all, rms_all = exchange(
-        sent, taps.reshape(seqs, replicas, SUB, LANES), jnp.full((1, LANES), top * (1.0 / TOP8), jnp.float32)
+    back, grad, rms = exchange(
+        seqs, dps, activations[0], gate_values[0], output_grad[0], filter_codes, filter_scales
     )
-    grad_all = grad_all.reshape(replicas // 2, 2, seqs, SUB, LANES).transpose(2, 0, 1, 3, 4).reshape(channels, SUB, LANES)
-    rms_all = rms_all.reshape(replicas // 2, 2, seqs, LANES).transpose(2, 0, 1, 3).reshape(channels, replicas, 2, -1)
-    rms_all = lax.dynamic_index_in_dim(rms_all[..., 0], lax.axis_index("dp"), 1, keepdims=False)
-
-    back = back.astype(jnp.float32)
-    conv = by_position(root_of(back[:, :SUB], 12) * (rms_all[:, 0] * (1.0 / TOP12))[:, None, None])
-    input_grad = by_position(root_of(back[:, SUB:], 8) * (rms_all[:, 1] * (1.0 / TOP8_RMS))[:, None, None])
-    gate_grad = (grad_in * conv).astype(jnp.bfloat16)
-    code_grad = by_position(grad_all) * scale_rows
+    input_grad, gate_grad, code_grad = finish(
+        dps, back, grad.reshape(channels // 2, 2 * SUB, LANES), rms.reshape(channels, 1, LANES), output_grad[0], filter_scales
+    )
     return (input_grad[None], gate_grad[None], code_grad)
 
 

time: 113 us -> 93.6 us (0.83)
  local copies, waits for them, and re-layouts: 14.6 us -> 0 us
  other arithmetic: 7.77 us -> 0 us
  Pallas kernels: 88.5 us -> 92.6 us
    unnamed x23 -> x0, local copies, waits for them, and re-layouts: 8.91 us -> none
    pallas_call x0 -> x1, Pallas kernels: none -> 8.01 us  [finish(): pl.pallas_call(functools.partial(finish_kernel, dps), grid=(SUB,), out_sh...]
    reshape x6 -> x0, local copies, waits for them, and re-layouts: 4.71 us -> none  [the longest x2 3.41 us: on_device(): rms_all.reshape(replicas // 2, 2, seqs, LANES).transpose(2, 0, 1, 3)]
    pallas_call x1, Pallas kernels: 88.5 us -> 84.6 us  [exchange(): pl.pallas_call(functools.partial(main_kernel, seqs, dps), out_shape=(jax....]
    mul x4 -> x0, other arithmetic: 2.47 us -> none  [the longest x1 1.34 us: on_device(): act_code = eighth_power(act * (TOP8 / top)).astype(jnp.bfloat16)]
    transpose x2 -> x0, other arithmetic: 2.11 us -> none  [the longest x1 1.87 us: by_position(): return value.transpose(1, 2, 0).reshape(SUB * LANES, value.shape[0])]
    reduce_max x1 -> x0, other arithmetic: 1.93 us -> none  [on_device(): top = jnp.maximum(jnp.max(jnp.abs(act)), FLOOR)]
where the time goes in v4:
time: 93.6 us; the launch traced here: 93.2 us
  Pallas kernels  92.6 us (99%)
    pallas_call x1, Pallas kernels, exchange(): pl.pallas_call(functools.partial(main_kernel, seqs, dps), out_shape=(jax....  84.6 us
    pallas_call x1, Pallas kernels, finish(): pl.pallas_call(functools.partial(finish_kernel, dps), grid=(SUB,), out_sh...  8.01 us

profile of v4, /device:TPU:1, one launch (start us, length us, event | category | flops | bytes accessed | tf_op | source)
XLA Modules:
  0.0 93.2 jit_solution(5388296794351542914)
XLA Ops:
  0.6 84.6 %shard_map.121 = (bf16[256,16,128]{2,1,0:T(8,128)(2,1)}, bf16[4,32,16,128]{3,2,1,0:T(8,128)(2,1)}, f32[4,64,1,128]{3,2,1,0:T(1,128)}) custom-call(bf16[1024,256]{1,0:T(8,128)(2,1)} %bitcast.9, bf16[1024,256]{1,0:T(8,128)(2,1)} %bitcast.10, bf16[1024,256]{1,0:T(8,128)(2,1)} %bitcast.7, bf16[1024,256]{1,0:T(8,128)(2,1)} %codes_hbm.1, ...), custom_call_target="tpu_custom_call" | custom-call | tf_op jit(solution)/shard_map/pallas_call | solution.py:412
  85.2 8.0 %shard_map.122 = (f32[1024,256]{1,0:T(8,128)}, bf16[1024,256]{1,0:T(8,128)(2,1)}, f32[1024,256]{1,0:T(8,128)}) custom-call(bf16[256,16,128]{2,1,0:T(8,128)(2,1)} %get-tuple-element.9.back_ref, bf16[128,16,128]{2,1,0:T(8,128)(2,1)} %bitcast.11, f32[256,1,128]{2,1,0:T(1,128)} %bitcast.12, bf16[1024,256]{1,0:T(8,128)(2,1)} %bitcast.8, f32[8,256]{1,0:T(8,128)} %filter_scale_ref.3), custom_call_target="tpu_custom_call" | custom-call | tf_op jit(solution)/shard_map/pallas_call | solution.py:491

commit v5 on v4

--- a/solution.py
+++ b/solution.py
@@ -135,37 +135,15 @@
     )
 
 
-def greet(seqs, dps, seq, dp, ready, meanwhile):
-    barrier = pltpu.get_barrier_semaphore()
-    chips = seqs // 2
-    core, chip = lax.rem(seq, 2), seq // 2
-    near = 2 * dps
-
-    def tell(sem, seq_to, dp_to):
-        pl.semaphore_signal(sem, inc=1, device_id={"seq": seq_to, "dp": dp_to}, device_id_type=pl.DeviceIdType.MESH)
-
-    def tell_near(offset, carry):
-        peer = lax.rem(core * dps + dp + offset, near)
-        tell(barrier, chip * 2 + peer // dps, lax.rem(peer, dps))
-        return carry
-
-    def tell_far(sem):
-        def body(offset, carry):
-            tell(sem, lax.rem(chip + offset, chips) * 2 + core, dp)
-            return carry
-
-        return body
-
-    lax.fori_loop(1, chips, tell_far(barrier), 0)
-    lax.fori_loop(1, near, tell_near, 0)
-    meanwhile()
-    pl.semaphore_wait(barrier, near + chips - 2)
-    lax.fori_loop(1, chips, tell_far(ready), 0)
-    pl.semaphore_wait(ready, chips - 1)
+def tell(sem, seq, dp):
+    pl.semaphore_signal(sem, inc=1, device_id={"seq": seq, "dp": dp}, device_id_type=pl.DeviceIdType.MESH)
 
 
 SCALE, TAPS, SCALES, GRAD, RMS, BACK, GRAD_Y, RMS_Y, DATA = range(9)
 CONV_LANE, GRAD_LANE, BACK_LANE = 0, 4, 8
+
+
+AHEAD = 3
 
 
 def lane_of(rows, lane, wanted):
@@ -178,7 +156,7 @@
     back_ref, grad_all_ref, rms_all_ref,
     acts_ref, gate_ref, cot_ref, codes_ref, first_ref, last_ref, forward_ref, backward_ref, twist_ref,
     turned, taps_ref, data_ref, scale_ref,
-    got, taps_got, scale_got, scale_row, scales_got, conv_specs, back_specs, cross_ref, out, grad, rms, held, held_rms,
+    got, taps_got, scale_got, scale_row, scales_got, cross_ref, out, grad, rms, held, held_rms,
     grad_code, send_sems, recv_sems, local_sems, load_sems, ready,
 ):
     seq, dp = lax.axis_index("seq"), lax.axis_index("dp")
@@ -243,13 +221,28 @@
     def taps_of(seq_to):
         return taps_ref.at[pl.ds(pl.multiple_of((dp * seqs + seq_to) * SUB, SUB), SUB)]
 
-    greet(seqs, dps, seq, dp, ready, turn)
+    barrier = pltpu.get_barrier_semaphore()
+
+    def tell_pair(offset, carry):
+        tell(barrier, lax.rem(seq + offset // 2, seqs), pair * 2 + lax.rem(parity + offset, 2))
+        return carry
+
+    def tell_others(sem):
+        def body(offset, carry):
+            tell(sem, seq, lax.rem(pair + offset, pairs) * 2 + parity)
+            return carry
+
+        return body
+
+    lax.fori_loop(1, pairs, tell_others(barrier), 0)
+    lax.fori_loop(1, 2 * seqs, tell_pair, 0)
+    turn()
+    pl.semaphore_wait(barrier, 2 * seqs + pairs - 2)
+    lax.fori_loop(1, pairs, tell_others(ready), 0)
 
     def send_scale(offset, carry):
         copy_to(scale_ref, scale_got.at[dp], SCALE, seq, lax.rem(dp + offset, dps)).start()
         return carry
-
-    lax.fori_loop(1, dps, send_scale, 0)
 
     def send_taps(offset, carry):
         peer = lax.rem(seq + offset, seqs)
@@ -267,13 +260,18 @@
             copy_to(source_of(peer_seq, peer_dp), target.at[mine], kind, peer_seq, peer_dp, recv_kind).start()
             return carry
 
-        lax.fori_loop(jnp.where(step == 0, 1, 0), 2 * seqs, send, 0)
-
-    def send_data(step, carry):
-        send_pair(step, lambda s, d: data_ref.at[d * seqs + s], got, DATA, DATA + pair)
-        return carry
-
-    lax.fori_loop(0, pairs, send_data, 0)
+        lax.fori_loop(jnp.where(lax.rem(step, pairs) == 0, 1, 0), 2 * seqs, send, 0)
+
+    def send_data(step):
+        send_pair(step, lambda s, d: data_ref.at[d * seqs + s], got, DATA + step, DATA + pair)
+
+    def sent_data(step, count):
+        of(got, count, DATA + step, DATA + step).wait_send()
+
+    send_data(0)
+    pl.semaphore_wait(ready, pairs - 1)
+    lax.fori_loop(1, dps, send_scale, 0)
+    lax.fori_loop(1, AHEAD, lambda step, carry: (send_data(step), carry)[1], 0)
     own = pltpu.make_async_copy(data_ref.at[mine], got.at[mine], local_sems.at[0])
     own.start()
     own_taps = pltpu.make_async_copy(taps_of(seq), taps_got.at[seq], local_sems.at[1])
@@ -305,12 +303,40 @@
     of(got, 2 * seqs - 1, DATA, DATA + pair).wait_recv()
     rms[...] = jnp.zeros_like(rms)
 
+    def send_back(step):
+        send_pair(pairs - step, lambda s, d: out.at[d, s], back_ref, BACK, BACK)
+
+    def send_grads():
+        cross = cross_ref[...]
+        grad_rms = jnp.maximum(root_mean_square(cross), RMS_FLOOR)
+        in_group = lane % group
+        rms[...] = jnp.where((in_group >= GRAD_LANE) & (in_group < BACK_LANE), grad_rms, rms[...])
+        (grad_value,) = inverse([cross], last_ref, backward_ref, twist_ref)
+        grad[...] = grad_value.reshape(seqs, SUB, LANES)
+
+        def send_grad(offset, carry):
+            peer_seq = lax.rem(seq + offset // 2, seqs)
+            peer_dp = pair * 2 + lax.rem(parity + offset, 2)
+            copy_to(grad.at[peer_seq], held.at[parity * seqs + seq], GRAD, peer_seq, peer_dp).start()
+            copy_to(rms, held_rms.at[parity * seqs + seq], RMS, peer_seq, peer_dp).start()
+            return carry
+
+        lax.fori_loop(1, 2 * seqs, send_grad, 0)
+
     def transform_pair(step, carry):
         source = lax.rem(pair + pairs - step, pairs)
 
         @pl.when(step > 0)
         def _():
             of(got, 2 * seqs, DATA, DATA + source).wait_recv()
+
+        @pl.when(step == 0)
+        def _():
+            sent_data(step, 2 * seqs - 1)
+
+        @pl.when(step < pairs - AHEAD)
+        def _():
+            send_data(step + AHEAD)
 
         signals, acts = [], []
         for half in range(2):
@@ -322,74 +348,57 @@
         act_high, act_low = halves(jnp.concatenate(acts, axis=1))
         signal_specs = forward(jnp.concatenate(signals, axis=1), None, first_ref, forward_ref, twist_ref)
         act_specs = forward(act_high, act_low, first_ref, forward_ref, twist_ref)
+        conv_specs, back_specs, factors = [], [], []
         for half, (signal_spec, act_spec) in enumerate(zip(signal_specs, act_specs)):
             index = source * 2 + half
             cross_ref[...] += times_conj(act_spec, signal_spec)
             conv_spec, back_spec = times(signal_spec, carry), times_conj(act_spec, carry)
-            conv_specs[index] = conv_spec
-            back_specs[index] = back_spec
+            conv_specs.append(conv_spec)
+            back_specs.append(back_spec)
             conv_rms = jnp.maximum(root_mean_square(conv_spec), RMS_FLOOR)
             back_rms = jnp.maximum(root_mean_square(back_spec), RMS_FLOOR)
+            factors.append((TOP14 / conv_rms, TOP8_RMS / back_rms))
             both = jnp.where(lane % group < BACK_LANE, conv_rms, back_rms)
             rms[...] = jnp.where(lane // group == index, both, rms[...])
+
+        @pl.when(step == pairs - 1)
+        def _():
+            send_grads()
+            send_back(1)
+            send_back(2)
+
+        convs = inverse(conv_specs, last_ref, backward_ref, twist_ref)
+        backs = inverse(back_specs, last_ref, backward_ref, twist_ref)
+        for half in range(2):
+            conv_code = fourteenth_power(convs[half] * factors[half][0]).reshape(seqs, SUB, LANES)
+            back_code = eighth_power(backs[half] * factors[half][1]).reshape(seqs, SUB, LANES)
+            out[source * 2 + half] = jnp.concatenate([conv_code, back_code], axis=1).astype(jnp.bfloat16)
+
+        @pl.when(step == 0)
+        def _():
+            send_back(step)
+
         return carry
 
     lax.fori_loop(0, pairs, transform_pair, taps_spec)
-
-    cross = cross_ref[...]
-    grad_rms = jnp.maximum(root_mean_square(cross), RMS_FLOOR)
-    in_group = lane % group
-    rms[...] = jnp.where((in_group >= GRAD_LANE) & (in_group < BACK_LANE), grad_rms, rms[...])
-    (grad_value,) = inverse([cross], last_ref, backward_ref, twist_ref)
-    grad[...] = grad_value.reshape(seqs, SUB, LANES)
-
-    def send_grad(offset, carry):
-        peer_seq = lax.rem(seq + offset // 2, seqs)
-        peer_dp = pair * 2 + lax.rem(parity + offset, 2)
-        copy_to(grad.at[peer_seq], held.at[parity * seqs + seq], GRAD, peer_seq, peer_dp).start()
-        copy_to(rms, held_rms.at[parity * seqs + seq], RMS, peer_seq, peer_dp).start()
-        return carry
-
-    lax.fori_loop(1, 2 * seqs, send_grad, 0)
-
-    def send_along_y():
-        of(held, 2 * seqs - 1, GRAD).wait()
-        of(held_rms, 2 * seqs - 1, RMS).wait()
-        held[parity * seqs + seq] = grad[seq]
-        held_rms[parity * seqs + seq] = rms[...]
-        code = eighth_power(held[...] * (TOP8_RMS / lane_of(held_rms[...], lane, GRAD_LANE)))
-        grad_code[...] = code.reshape(seqs, 2 * SUB, LANES).astype(jnp.bfloat16)
-
-        def send_along(offset, carry):
-            peer_dp = lax.rem(pair + offset, pairs) * 2 + parity
-            copy_to(grad_code, grad_all_ref.at[pair], GRAD_Y, seq, peer_dp).start()
-            copy_to(held_rms, rms_all_ref.at[pair], RMS_Y, seq, peer_dp).start()
-            return carry
-
-        lax.fori_loop(1, pairs, send_along, 0)
-
-    def invert_pair(step, carry):
-        target = lax.rem(pair + step, pairs)
-        convs = inverse([conv_specs[target * 2], conv_specs[target * 2 + 1]], last_ref, backward_ref, twist_ref)
-        backs = inverse([back_specs[target * 2], back_specs[target * 2 + 1]], last_ref, backward_ref, twist_ref)
-        for half in range(2):
-            index = target * 2 + half
-            conv_rms = lane_of(rms[...], lane, index * group + CONV_LANE)
-            back_rms = lane_of(rms[...], lane, index * group + BACK_LANE)
-            conv_code = fourteenth_power(convs[half] * (TOP14 / conv_rms)).reshape(seqs, SUB, LANES)
-            back_code = eighth_power(backs[half] * (TOP8_RMS / back_rms)).reshape(seqs, SUB, LANES)
-            out[index] = jnp.concatenate([conv_code, back_code], axis=1).astype(jnp.bfloat16)
-
-        @pl.when(step == 1)
-        def _():
-            send_along_y()
-
-        send_pair(step, lambda s, d: out.at[d, s], back_ref, BACK, BACK)
-        return carry
-
-    lax.fori_loop(0, pairs, invert_pair, 0)
     own_back = pltpu.make_async_copy(out.at[dp, seq], back_ref.at[mine], local_sems.at[0])
     own_back.start()
+
+    of(held, 2 * seqs - 1, GRAD).wait()
+    of(held_rms, 2 * seqs - 1, RMS).wait()
+    held[parity * seqs + seq] = grad[seq]
+    held_rms[parity * seqs + seq] = rms[...]
+    code = eighth_power(held[...] * (TOP8_RMS / lane_of(held_rms[...], lane, GRAD_LANE)))
+    grad_code[...] = code.reshape(seqs, 2 * SUB, LANES).astype(jnp.bfloat16)
+
+    def send_along(offset, carry):
+        peer_dp = lax.rem(pair + offset, pairs) * 2 + parity
+        copy_to(grad_code, grad_all_ref.at[pair], GRAD_Y, seq, peer_dp).start()
+        copy_to(held_rms, rms_all_ref.at[pair], RMS_Y, seq, peer_dp).start()
+        return carry
+
+    lax.fori_loop(1, pairs, send_along, 0)
+    lax.fori_loop(3, pairs, lambda step, carry: (send_back(step), carry)[1], 0)
     own_grad = pltpu.make_async_copy(grad_code, grad_all_ref.at[pair], local_sems.at[1])
     own_grad.start()
     own_rms = pltpu.make_async_copy(held_rms, rms_all_ref.at[pair], local_sems.at[2])
@@ -397,7 +406,7 @@
     own_back.wait()
     own_grad.wait()
     own_rms.wait()
-    of(got, channels - 1, DATA).wait_send()
+    lax.fori_loop(pairs - AHEAD, pairs, lambda step, carry: (sent_data(step, 2 * seqs), carry)[1], 0)
     of(grad_all_ref, pairs - 1, GRAD_Y).wait()
     of(rms_all_ref, pairs - 1, RMS_Y).wait()
     of(back_ref, channels - 1, BACK).wait()
@@ -430,8 +439,6 @@
             pltpu.VMEM((dps, 1, LANES), f32),
             pltpu.VMEM((1, LANES), f32),
             pltpu.VMEM((seqs, 1, LANES), f32),
-            pltpu.VMEM((dps, ROWS, 2 * LANES), f32),
-            pltpu.VMEM((dps, ROWS, 2 * LANES), f32),
             pltpu.VMEM((ROWS, 2 * LANES), f32),
             pltpu.VMEM((dps, seqs, 2 * SUB, LANES), bf16),
             pltpu.VMEM((seqs, SUB, LANES), f32),
@@ -439,7 +446,7 @@
             pltpu.VMEM((2 * seqs, SUB, LANES), f32),
             pltpu.VMEM((2 * seqs, 1, LANES), f32),
             pltpu.VMEM((seqs, 2 * SUB, LANES), bf16),
-            pltpu.SemaphoreType.DMA((DATA + 1,)),
+            pltpu.SemaphoreType.DMA((DATA + pairs,)),
             pltpu.SemaphoreType.DMA((DATA + pairs,)),
             pltpu.SemaphoreType.DMA((3,)),
             pltpu.SemaphoreType.DMA((9,)),

time: 93.6 us -> 91.3 us (0.975)
  Pallas kernels: 92.6 us -> 90.2 us
    pallas_call x1, Pallas kernels: 84.6 us -> 82.2 us  [exchange(): pl.pallas_call(functools.partial(main_kernel, seqs, dps), out_shape=(jax....]
where the time goes in v5:
time: 91.3 us; the launch traced here: 90.9 us
  Pallas kernels  90.2 us (99%)
    pallas_call x1, Pallas kernels, exchange(): pl.pallas_call(functools.partial(main_kernel, seqs, dps), out_shape=(jax....  82.2 us
    pallas_call x1, Pallas kernels, finish(): pl.pallas_call(functools.partial(finish_kernel, dps), grid=(SUB,), out_sh...  8.01 us

profile of v5, /device:TPU:1, one launch (start us, length us, event | category | flops | bytes accessed | tf_op | source)
XLA Modules:
  0.0 90.9 jit_solution(2734779307852061660)
XLA Ops:
  0.6 82.2 %shard_map.121 = (bf16[256,16,128]{2,1,0:T(8,128)(2,1)}, bf16[4,32,16,128]{3,2,1,0:T(8,128)(2,1)}, f32[4,64,1,128]{3,2,1,0:T(1,128)}) custom-call(bf16[1024,256]{1,0:T(8,128)(2,1)} %bitcast.9, bf16[1024,256]{1,0:T(8,128)(2,1)} %bitcast.10, bf16[1024,256]{1,0:T(8,128)(2,1)} %bitcast.7, bf16[1024,256]{1,0:T(8,128)(2,1)} %codes_hbm.1, ...), custom_call_target="tpu_custom_call" | custom-call | tf_op jit(solution)/shard_map/pallas_call | solution.py:421
  82.9 8.0 %shard_map.122 = (f32[1024,256]{1,0:T(8,128)}, bf16[1024,256]{1,0:T(8,128)(2,1)}, f32[1024,256]{1,0:T(8,128)}) custom-call(bf16[256,16,128]{2,1,0:T(8,128)(2,1)} %get-tuple-element.9.back_ref, bf16[128,16,128]{2,1,0:T(8,128)(2,1)} %bitcast.11, f32[256,1,128]{2,1,0:T(1,128)} %bitcast.12, bf16[1024,256]{1,0:T(8,128)(2,1)} %bitcast.8, f32[8,256]{1,0:T(8,128)} %filter_scale_ref.3), custom_call_target="tpu_custom_call" | custom-call | tf_op jit(solution)/shard_map/pallas_call | solution.py:498

commit v6 on v5

--- a/solution.py
+++ b/solution.py
@@ -144,6 +144,9 @@
 
 
 AHEAD = 3
+
+
+BLOCK = 32
 
 
 def lane_of(rows, lane, wanted):
@@ -456,58 +459,54 @@
     )(acts, gate, cot, codes, filter_scales, first, last, forward_table, backward_table, twist)
 
 
-def finish_kernel(dps, back_ref, grad_ref, rms_ref, cot_ref, filter_scale_ref, input_ref, gate_ref, code_ref, turned, turned_grad):
-    step = pl.program_id(0)
-    channels = back_ref.shape[0]
-    block = channels // dps
-
-    @pl.when(step == 0)
-    def _():
-        lane = lax.broadcasted_iota(jnp.int32, (1, LANES), 1)
-        base = lax.axis_index("dp") * (LANES // dps)
-
-        def decode(i, carry):
-            at = pl.ds(i * block, block)
-            rms = rms_ref[at]
-            tile = back_ref[at].astype(jnp.float32)
-            conv = root_of(tile[:, :SUB], 14) * (lane_of(rms, lane, base + CONV_LANE) * (1.0 / TOP14))
-            back = root_of(tile[:, SUB:], 8) * (lane_of(rms, lane, base + BACK_LANE) * (1.0 / TOP8_RMS))
-            rows = pl.ds(pl.multiple_of(i * block * 2 * SUB, 2 * SUB), block * 2 * SUB)
-            turned[rows] = jnp.concatenate([conv, back], axis=1).reshape(block * 2 * SUB, LANES)
-            grad = grad_ref[pl.ds(i * (block // 2), block // 2)].astype(jnp.float32).reshape(block, SUB, LANES)
-            grad = root_of(grad, 8) * (lane_of(rms, lane, GRAD_LANE) * (1.0 / TOP8_RMS))
-            turned_grad[pl.ds(pl.multiple_of(i * block * SUB, SUB), block * SUB)] = grad.reshape(block * SUB, LANES)
-            return carry
-
-        lax.fori_loop(0, dps, decode, 0)
-
-    scales = filter_scale_ref[pl.ds(step, 1)]
-    for start in range(0, channels, LANES):
-        part = slice(start, start + LANES)
-        conv = turned[pl.ds(start * 2 * SUB + step, LANES, stride=2 * SUB)].T
-        gate_ref[:, part] = (cot_ref[:, part].astype(jnp.float32) * conv).astype(jnp.bfloat16)
-        input_ref[:, part] = turned[pl.ds(start * 2 * SUB + SUB + step, LANES, stride=2 * SUB)].T
-        grad = turned_grad[pl.ds(start * SUB + step, LANES, stride=SUB)].T
-        code_ref[:, part] = grad * scales[:, part]
+def finish_kernel(dps, block, back_ref, grad_ref, rms_ref, cot_ref, filter_scale_ref, input_ref, gate_ref, code_ref, turned, turned_grad):
+    lane = lax.broadcasted_iota(jnp.int32, (1, LANES), 1)
+    base = lax.axis_index("dp") * (LANES // dps)
+
+    def decode(i, carry):
+        at = pl.ds(i * block, block)
+        rms = rms_ref[at]
+        tile = back_ref[at].astype(jnp.float32)
+        conv = root_of(tile[:, :SUB], 14) * (lane_of(rms, lane, base + CONV_LANE) * (1.0 / TOP14))
+        back = root_of(tile[:, SUB:], 8) * (lane_of(rms, lane, base + BACK_LANE) * (1.0 / TOP8_RMS))
+        rows = pl.ds(pl.multiple_of(i * block * 2 * SUB, 2 * SUB), block * 2 * SUB)
+        turned[rows] = jnp.concatenate([conv, back], axis=1).reshape(block * 2 * SUB, LANES)
+        grad = grad_ref[pl.ds(i * (block // 2), block // 2)].astype(jnp.float32).reshape(block, SUB, LANES)
+        grad = root_of(grad, 8) * (lane_of(rms, lane, GRAD_LANE) * (1.0 / TOP8_RMS))
+        turned_grad[pl.ds(pl.multiple_of(i * block * SUB, SUB), block * SUB)] = grad.reshape(block * SUB, LANES)
+        return carry
+
+    lax.fori_loop(0, LANES // block, decode, 0)
+    for i in range(SUB):
+        rows = slice(i * LANES, (i + 1) * LANES)
+        conv = turned[pl.ds(i, LANES, stride=2 * SUB)].T
+        gate_ref[rows] = (cot_ref[rows].astype(jnp.float32) * conv).astype(jnp.bfloat16)
+        input_ref[rows] = turned[pl.ds(SUB + i, LANES, stride=2 * SUB)].T
+        code_ref[rows] = turned_grad[pl.ds(i, LANES, stride=SUB)].T * filter_scale_ref[i : i + 1]
 
 
 def finish(dps, back, grad, rms, cot, filter_scales):
-    channels = back.shape[0]
-    vmem = pl.BlockSpec(memory_space=pltpu.VMEM)
-    chunk = pl.BlockSpec((LANES, channels), lambda i: (i, 0))
+    positions, channels = cot.shape
+    part = pl.BlockSpec((positions, LANES), lambda i: (0, i))
     return pl.pallas_call(
-        functools.partial(finish_kernel, dps),
-        grid=(SUB,),
+        functools.partial(finish_kernel, dps, BLOCK),
+        grid=(channels // LANES,),
         out_shape=(
             jax.ShapeDtypeStruct(cot.shape, jnp.float32),
             jax.ShapeDtypeStruct(cot.shape, jnp.bfloat16),
             jax.ShapeDtypeStruct(cot.shape, jnp.float32),
         ),
-        in_specs=[vmem, vmem, vmem, chunk, vmem],
-        out_specs=(chunk,) * 3,
+        in_specs=[
+            pl.BlockSpec((LANES, 2 * SUB, LANES), lambda i: (i, 0, 0)),
+            pl.BlockSpec((LANES // 2, 2 * SUB, LANES), lambda i: (i, 0, 0)),
+            pl.BlockSpec((LANES, 1, LANES), lambda i: (i, 0, 0)),
+            part,
+            pl.BlockSpec((SUB, LANES), lambda i: (0, i)),
+        ],
+        out_specs=(part,) * 3,
         scratch_shapes=[
-            pltpu.VMEM((channels * 2 * SUB, LANES), jnp.float32),
-            pltpu.VMEM((channels * SUB, LANES), jnp.float32),
+            pltpu.VMEM((LANES * 2 * SUB, LANES), jnp.float32),
+            pltpu.VMEM((LANES * SUB, LANES), jnp.float32),
         ],
         compiler_params=pltpu.CompilerParams(vmem_limit_bytes=62 << 20),
     )(back, grad, rms, cot, filter_scales)

time: 91.3 us -> 87.9 us (0.963)
  Pallas kernels: 90.2 us -> 87.1 us
    pallas_call x1, Pallas kernels: 8.01 us -> 4.89 us  [finish(): pl.pallas_call(functools.partial(finish_kernel, dps, BLOCK), grid=(channe...]
where the time goes in v6:
time: 87.9 us; the launch traced here: 87.8 us
  Pallas kernels  87.1 us (99%)
    pallas_call x1, Pallas kernels, exchange(): pl.pallas_call(functools.partial(main_kernel, seqs, dps), out_shape=(jax....  82.2 us
    pallas_call x1, Pallas kernels, finish(): pl.pallas_call(functools.partial(finish_kernel, dps, BLOCK), grid=(channe...  4.89 us

profile of v6, /device:TPU:1, one launch (start us, length us, event | category | flops | bytes accessed | tf_op | source)
XLA Modules:
  0.0 87.8 jit_solution(2395495644238159664)
XLA Ops:
  0.6 82.2 %shard_map.121 = (bf16[256,16,128]{2,1,0:T(8,128)(2,1)}, bf16[4,32,16,128]{3,2,1,0:T(8,128)(2,1)}, f32[4,64,1,128]{3,2,1,0:T(1,128)}) custom-call(bf16[1024,256]{1,0:T(8,128)(2,1)} %bitcast.9, bf16[1024,256]{1,0:T(8,128)(2,1)} %bitcast.10, bf16[1024,256]{1,0:T(8,128)(2,1)} %bitcast.7, bf16[1024,256]{1,0:T(8,128)(2,1)} %codes_hbm.1, ...), custom_call_target="tpu_custom_call" | custom-call | tf_op jit(solution)/shard_map/pallas_call | solution.py:424
  82.9 4.9 %shard_map.122 = (f32[1024,256]{1,0:T(8,128)}, bf16[1024,256]{1,0:T(8,128)(2,1)}, f32[1024,256]{1,0:T(8,128)}) custom-call(bf16[256,16,128]{2,1,0:T(8,128)(2,1)} %get-tuple-element.9.back_ref, bf16[128,16,128]{2,1,0:T(8,128)(2,1)} %bitcast.11, f32[256,1,128]{2,1,0:T(1,128)} %bitcast.12, bf16[1024,256]{1,0:T(8,128)(2,1)} %bitcast.8, f32[8,256]{1,0:T(8,128)} %filter_scale_ref.3), custom_call_target="tpu_custom_call" | custom-call | tf_op jit(solution)/shard_map/pallas_call | solution.py:491

commit v7 on v6

--- a/solution.py
+++ b/solution.py
@@ -221,8 +221,8 @@
         part = ref.at[pl.ds(0, count)]
         return copy_to(part, part, kind, next_seq, dp, recv_kind)
 
-    def taps_of(seq_to):
-        return taps_ref.at[pl.ds(pl.multiple_of((dp * seqs + seq_to) * SUB, SUB), SUB)]
+    def taps_of(seq_to, dp_to):
+        return taps_ref.at[pl.ds(pl.multiple_of((dp_to * seqs + seq_to) * SUB, SUB), SUB)]
 
     barrier = pltpu.get_barrier_semaphore()
 
@@ -249,7 +249,9 @@
 
     def send_taps(offset, carry):
         peer = lax.rem(seq + offset, seqs)
-        copy_to(taps_of(peer), taps_got.at[seq], TAPS, peer, dp).start()
+        apart = lax.rem(seq // 2, 4) - lax.rem(peer // 2, 4)
+        dp_to = pair * 2 + lax.rem(parity + apart * apart // 9, 2)
+        copy_to(taps_of(peer, dp_to), taps_got.at[seq], TAPS, peer, dp_to).start()
         return carry
 
     lax.fori_loop(1, seqs, send_taps, 0)
@@ -277,7 +279,7 @@
     lax.fori_loop(1, AHEAD, lambda step, carry: (send_data(step), carry)[1], 0)
     own = pltpu.make_async_copy(data_ref.at[mine], got.at[mine], local_sems.at[0])
     own.start()
-    own_taps = pltpu.make_async_copy(taps_of(seq), taps_got.at[seq], local_sems.at[1])
+    own_taps = pltpu.make_async_copy(taps_of(seq, dp), taps_got.at[seq], local_sems.at[1])
     own_taps.start()
 
     of(scale_got, dps - 1, SCALE).wait()

time: 87.9 us -> 87.6 us (level)
  no operation moved by 1% of the time
where the time goes in v7:
time: 87.6 us; the launch traced here: 87.5 us
  Pallas kernels  86.8 us (99%)
    pallas_call x1, Pallas kernels, exchange(): pl.pallas_call(functools.partial(main_kernel, seqs, dps), out_shape=(jax....  81.9 us
    pallas_call x1, Pallas kernels, finish(): pl.pallas_call(functools.partial(finish_kernel, dps, BLOCK), grid=(channe...  4.89 us

profile of v7, /device:TPU:1, one launch (start us, length us, event | category | flops | bytes accessed | tf_op | source)
XLA Modules:
  0.0 87.5 jit_solution(14533516975038363170)
XLA Ops:
  0.6 81.9 %shard_map.121 = (bf16[256,16,128]{2,1,0:T(8,128)(2,1)}, bf16[4,32,16,128]{3,2,1,0:T(8,128)(2,1)}, f32[4,64,1,128]{3,2,1,0:T(1,128)}) custom-call(bf16[1024,256]{1,0:T(8,128)(2,1)} %bitcast.9, bf16[1024,256]{1,0:T(8,128)(2,1)} %bitcast.10, bf16[1024,256]{1,0:T(8,128)(2,1)} %bitcast.7, bf16[1024,256]{1,0:T(8,128)(2,1)} %codes_hbm.1, ...), custom_call_target="tpu_custom_call" | custom-call | tf_op jit(solution)/shard_map/pallas_call | solution.py:426
  82.6 4.9 %shard_map.122 = (f32[1024,256]{1,0:T(8,128)}, bf16[1024,256]{1,0:T(8,128)(2,1)}, f32[1024,256]{1,0:T(8,128)}) custom-call(bf16[256,16,128]{2,1,0:T(8,128)(2,1)} %get-tuple-element.9.back_ref, bf16[128,16,128]{2,1,0:T(8,128)(2,1)} %bitcast.11, f32[256,1,128]{2,1,0:T(1,128)} %bitcast.12, bf16[1024,256]{1,0:T(8,128)(2,1)} %bitcast.8, f32[8,256]{1,0:T(8,128)} %filter_scale_ref.3), custom_call_target="tpu_custom_call" | custom-call | tf_op jit(solution)/shard_map/pallas_call | solution.py:493
